TPU v7x, 32 devices: a whole 2x2x4 slice. The times are simulated.
32 devices in a mesh: seq: 4 (over z), dp: 8 (over y, x, core).
Axes of the slice: x: 2, y: 2, z: 4, core: 2. Of those that a mesh axis runs over, the one named last changes fastest.
Arguments:
- tokens: bfloat16 [64, 1024, 640], P('dp', 'seq'), may hold values from -6 to 6
- weights: bfloat16 [1280, 1920], P(('seq', 'dp')), may hold values from -0.15625 to 0.15625
- bias: float32 [1920], replicated, may hold values from -3 to 9
- resets: int32 [64, 1024], P('dp', 'seq'), may hold values from 0 to 1, as said below
- upstream: bfloat16 [64, 1024, 640], P('dp', 'seq'), may hold values from -6 to 6
Outputs:
- hidden: bfloat16 [64, 1024, 640], P('dp', 'seq')
- grad_tokens: bfloat16 [64, 1024, 640], P('dp', 'seq')
- grad_weights: float32 [1280, 1920], P(('seq', 'dp'))
- grad_bias: float32 [1920], replicated
Inputs may be any that keep to these rules, and one draw needn't show every extreme that they name: In each group of 8 sequences of one dp index, one sequence, drawn from the seed, has no resets; the others may have resets at uneven places.
All inputs are finite; a program needn't handle non-finite values.
Results may differ from a plain program's by a relative error of at most 0.0049.
Values may be sent and summed in bfloat16 or wider, within the bound.
A program may use at most 128 MiB of HBM per device.

v0:
```python
import math

import jax
import jax.numpy as jnp
from jax import lax
from jax.sharding import PartitionSpec as P


def from_behind(shard, axis, by):
    count = lax.axis_size(axis)
    pairs = [(i, i + by) for i in range(count) if 0 <= i + by < count]
    return lax.ppermute(shard, axis, pairs)


def chain_pool(factor, source, reverse):
    seq_count, span_len, width = factor.shape
    block_len = math.gcd(8, span_len)
    block_count = span_len // block_len
    flat_factor = factor.reshape(seq_count * block_count, block_len * width)
    flat_source = source.reshape(seq_count * block_count, block_len * width)
    gain_run = jnp.ones((seq_count * block_count, width), jnp.float32)
    state_run = jnp.zeros((seq_count * block_count, width), jnp.float32)
    gain_list = [None] * block_len
    state_list = [None] * block_len
    order = range(block_len - 1, -1, -1) if reverse else range(block_len)
    for index in order:
        factor_now = flat_factor[:, index * width : (index + 1) * width]
        source_now = flat_source[:, index * width : (index + 1) * width]
        gain_run = gain_run * factor_now
        state_run = factor_now * state_run + source_now
        gain_list[index] = gain_run
        state_list[index] = state_run
    block_gains = jnp.concatenate(gain_list, axis=1).reshape(
        seq_count, block_count, block_len, width
    )
    block_states = jnp.concatenate(state_list, axis=1).reshape(
        seq_count, block_count, block_len, width
    )
    total_gain = jnp.transpose(gain_run.reshape(seq_count, block_count, width), (1, 0, 2))
    total_state = jnp.transpose(state_run.reshape(seq_count, block_count, width), (1, 0, 2))

    def advance(carry, item):
        gain_prev, state_prev = carry
        gain_here, state_here = item
        return (
            (gain_prev * gain_here, gain_here * state_prev + state_here),
            (gain_prev, state_prev),
        )

    start = (jnp.ones((seq_count, width), jnp.float32), jnp.zeros((seq_count, width), jnp.float32))
    ignored, entering = lax.scan(advance, start, (total_gain, total_state), reverse=reverse)
    gain_in = jnp.transpose(entering[0], (1, 0, 2))[:, :, None, :]
    state_in = jnp.transpose(entering[1], (1, 0, 2))[:, :, None, :]
    gains = (block_gains * gain_in).reshape(seq_count, span_len, width)
    states = (block_states + block_gains * state_in).reshape(seq_count, span_len, width)
    return (gains, states)


def per_device(tokens, weights, bias, resets, upstream):
    seq_count, span_len, model_width = tokens.shape
    row_count = seq_count * span_len
    keep_mask = (1 - resets).astype(jnp.float32)[..., None]
    left_rows = from_behind(tokens[:, -1, :], "seq", 1)
    shifted = jnp.concatenate([left_rows[:, None, :], tokens[:, :-1, :]], axis=1)
    shifted = jnp.where(resets[..., None] == 1, jnp.zeros_like(shifted), shifted)
    joined = jnp.concatenate([tokens, shifted], axis=2).reshape(row_count, 2 * model_width)
    columns = joined
    preact = (
        jnp.dot(
            columns,
            lax.all_gather(weights, ("seq", "dp"), axis=0, tiled=True),
            preferred_element_type=jnp.float32,
        )
        + bias
    )
    preact = preact.reshape(seq_count, span_len, 3 * model_width)
    z_gate = jnp.tanh(preact[..., :model_width])
    f_gate = jax.nn.sigmoid(preact[..., model_width : 2 * model_width])
    o_gate = jax.nn.sigmoid(preact[..., 2 * model_width :])
    effective = f_gate * keep_mask
    fresh = (1 - f_gate) * z_gate
    gains, local_cell = chain_pool(effective, fresh, False)
    total_gain = gains[:, -1]
    local_end = local_cell[:, -1]

    def relay_step(index, value):
        return from_behind(local_end + total_gain * value, "seq", 1)

    carry_in = lax.fori_loop(0, lax.axis_size("seq") - 1, relay_step, jnp.zeros_like(local_end))
    cell_state = local_cell + gains * carry_in[:, None, :]
    hidden = (o_gate * cell_state).astype(jnp.bfloat16)
    grad_out = upstream.astype(jnp.float32)
    grad_o = grad_out * cell_state
    source = grad_out * o_gate
    next_eff = jnp.concatenate([effective[:, 1:], jnp.ones_like(effective[:, :1])], axis=1)
    back_gain, back_local = chain_pool(next_eff, source, True)
    send_value = effective[:, 0] * back_local[:, 0]

    def back_step(index, value):
        return from_behind(send_value + total_gain * value, "seq", -1)

    back_in = lax.fori_loop(0, lax.axis_size("seq") - 1, back_step, jnp.zeros_like(send_value))
    grad_cell = back_local + back_gain * back_in[:, None, :]
    before = jnp.concatenate([carry_in[:, None, :], cell_state[:, :-1]], axis=1)
    grad_f = grad_cell * before * keep_mask - grad_cell * z_gate
    grad_z = grad_cell * (1 - f_gate)
    grad_pre = jnp.concatenate(
        [
            grad_z * (1 - z_gate * z_gate),
            grad_f * f_gate * (1 - f_gate),
            grad_o * o_gate * (1 - o_gate),
        ],
        axis=2,
    )
    grad_pre = grad_pre.reshape(row_count, 3 * model_width).astype(jnp.bfloat16)
    grad_bias = lax.psum(jnp.sum(grad_pre, axis=0, dtype=jnp.float32), ("seq", "dp"))
    grad_joined = lax.dot_general(
        grad_pre,
        lax.all_gather(weights, ("seq", "dp"), axis=0, tiled=True),
        (((1,), (1,)), ((), ())),
        preferred_element_type=jnp.float32,
    )
    grad_joined = grad_joined.reshape(seq_count, span_len, 2 * model_width)
    grad_prev = grad_joined[..., model_width:] * keep_mask
    incoming = from_behind(grad_prev[:, 0, :], "seq", -1)
    later_rows = jnp.concatenate([grad_prev[:, 1:], incoming[:, None, :]], axis=1)
    grad_tokens = (grad_joined[..., :model_width] + later_rows).astype(jnp.bfloat16)
    columns = joined
    grad_weights = lax.psum_scatter(
        lax.dot_general(
            columns, grad_pre, (((0,), (0,)), ((), ())), preferred_element_type=jnp.float32
        ),
        ("seq", "dp"),
        scatter_dimension=0,
        tiled=True,
    )
    return (hidden, grad_tokens, grad_weights, grad_bias)


def solution(mesh):
    placed = (
        P("dp", "seq", None),
        P(("seq", "dp"), None),
        P(),
        P("dp", "seq"),
        P("dp", "seq", None),
    )
    return jax.shard_map(
        per_device,
        mesh=mesh,
        in_specs=placed,
        out_specs=(P("dp", "seq", None), P("dp", "seq", None), P(("seq", "dp"), None), P()),
        check_vma=False,
    )
```

profile of v0, /device:TPU:0, one launch (start us, length us, event | category | flops | bytes accessed | tf_op | source)
XLA Modules:
  0.0 547.0 jit_solution(6675215902481062290)
XLA Ops:
  8.9 4.9 collective-permute-start.2
  15.2 3.0 copy.34
  18.2 1.5 copy.33
  19.8 2.6 maximum_select_fusion
  22.4 1.5 copy-done.9
  24.0 2.7 pad_maximum_fusion.1
  26.6 7.9 %copy.35 = bf16[8,256,1280]{2,1,0:T(8,128)(2,1)} copy(bf16[8,256,1280]{1,2,0:T(8,128)(2,1)} %pad_maximum_fusion.1) | data formatting | bytes 10485760 | tf_op jit(solution)/shard_map/concatenate | solution.py:66
  34.5 43.5 %all-gather.2.cloned.1.call-done = bf16[1280,1920]{1,0:T(8,128)(2,1)} async-done(((bf16[40,1920]{1,0:T(8,128)(2,1)}), bf16[1280,1920]{1,0:T(8,128)(2,1)}) %all-gather.2.cloned.1.call-update) | async-done | bytes 4915216 | tf_op jit(solution)/shard_map/all_gather | solution.py:71
  78.0 14.4 %broadcast_add_fusion = f32[2048,1920]{1,0:T(8,128)S(1)} fusion(f32[1920]{0:T(1024)S(1)} %copy-done.16, bf16[2048,1280]{1,0:T(8,128)(2,1)} %bitcast.111, bf16[1280,1920]{1,0:T(8,128)(2,1)} %all-gather.2.cloned.1.call-done), kind=kOutput, calls=%fused_computation.21 | convolution fusion | flops 10070261760 | bytes 25894400 | tf_op jit(solution)/shard_map/dot_general | solution.py:69
  92.4 5.5 %broadcast_multiply_fusion = (f32[8,256,640]{2,1,0:T(8,128)}, f32[8,256,640]{2,1,0:T(8,128)}) fusion(f32[8,256]{1,0:T(8,128)S(1)} %subtract_convert_fusion, f32[8,256,1920]{2,1,0:T(8,128)S(1)} %bitcast.102), kind=kLoop, calls=%fused_computation.61 | loop fusion | flops 7864320 | bytes 20979712 | tf_op jit(solution)/shard_map/mul | solution.py:80
  98.0 3.0 copy-done.1
  101.0 6.4 %reshape.81 = f32[256,5120]{1,0:T(8,128)} reshape(f32[8,256,640]{2,1,0:T(8,128)} %get-tuple-element.395) | data formatting | bytes 10485760 | tf_op jit(solution)/shard_map/reshape | solution.py:19
  107.3 5.2 slice.210
  112.6 6.3 %reshape.82 = f32[256,5120]{1,0:T(8,128)} reshape(f32[8,256,640]{2,1,0:T(8,128)} %get-tuple-element.396) | data formatting | bytes 10485760 | tf_op jit(solution)/shard_map/reshape | solution.py:20
  118.9 1.6 slice_dynamic-update-slice_fusion.1
  120.5 2.0 constant_dynamic-update-slice_fusion.6
  122.6 2.5 fusion.25
  126.3 1.4 constant_dynamic-update-slice_fusion.7
  127.7 2.3 copy-done.12
  130.1 2.4 copy-done.13
  133.4 53.6 %while.60 = (s32[]{:T(128)}, f32[8,640]{1,0:T(8,128)S(1)}, f32[8,640]{1,0:T(8,128)S(1)}, f32[32,8,640]{2,1,0:T(8,128)S(1)}, f32[32,8,640]{2,1,0:T(8,128)}, /*ind...) while((s32[]{:T(128)}, f32[8,640]{1,0:T(8,128)S(1)}, ...), condition=%wide.region_1.2_spmd.clone, body=%wide.region_0.1_spmd.clone.sunk | while | flops 35843 | bytes 287340 | solution.py:51
  189.1 2.1 copy.39
  191.1 6.3 %reshape.83 = f32[8,256,640]{2,1,0:T(8,128)} reshape(f32[256,5120]{1,0:T(8,128)} %copy-done.13) | data formatting | bytes 10485760 | tf_op jit(solution)/shard_map/reshape | solution.py:36
  197.4 6.4 %reshape.84 = f32[8,256,640]{2,1,0:T(8,128)} reshape(f32[256,5120]{1,0:T(8,128)} %copy-done.12) | data formatting | bytes 10485760 | tf_op jit(solution)/shard_map/reshape | solution.py:33
  203.8 4.8 bitcast_multiply_fusion.2
  208.7 2.3 copy-done.4
  211.0 1.6 copy-done.5
  212.7 16.6 %while.58 = (s32[]{:T(128)}, f32[8,640]{1,0:T(8,128)S(1)}, f32[8,640]{1,0:T(8,128)S(1)}, f32[8,640]{1,0:T(8,128)S(1)}, s32[]{:T(128)}) while((s32[]{:T(128)}, f32[8,640]{1,0:T(8,128)S(1)}, f32[8,640]{1,0:T(8,128)S(1)}, f32[8,640]{1,0:T(8,128)S(1)}, s32[]{:T(128)}) %tuple.147), condition=%wide.region_3.4_spmd, body=%wide.region_2.3_spmd.sunk | while | flops 10242 | bytes 163941 | solution.py:89
  212.7 3.8 collective-permute-start
  216.5 1.5 collective-permute-done
  218.0 4.2 collective-permute-start
  222.2 1.5 collective-permute-done
  223.7 4.2 collective-permute-start
  227.9 1.5 collective-permute-done
  229.3 11.2 %fusion.6 = (bf16[8,256,640]{2,1,0:T(8,128)(2,1)}, f32[8,256,640]{2,1,0:T(8,128)}, f32[8,256,640]{2,1,0:T(8,128)}) fusion(bf16[8,256,640]{2,1,0:T(8,128)(2,1)} %param.17, f32[8,256,1920]{2,1,0:T(8,128)} %bitcast.103, f32[8,256,640]{2,1,0:T(8,128)} %copy-done.5, f32[8,256,640]{2,1,0:T(8,128)} %copy-done.4, f32[8,640]{1,0:T(8,128)S(1)} %get-tuple-element.230), kind=kLoop, calls=%fused_computation.26 | loop fusion | flops 15728640 | bytes 31477760 | tf_op jit(solution)/shard_map/convert.2
  240.6 6.4 %reshape.88 = f32[256,5120]{1,0:T(8,128)} reshape(f32[8,256,640]{2,1,0:T(8,128)} %get-tuple-element.393) | data formatting | bytes 10485760 | tf_op jit(solution)/shard_map/reshape | solution.py:20
  246.9 5.2 concatenate.35
  252.1 6.3 %reshape.87 = f32[256,5120]{1,0:T(8,128)} reshape(f32[8,256,640]{2,1,0:T(8,128)} %concatenate.35) | data formatting | bytes 10485760 | tf_op jit(solution)/shard_map/reshape | solution.py:19
  258.4 3.7 constant_dynamic-update-slice_fusion.21
  262.7 4.1 constant_dynamic-update-slice_fusion.17
  268.2 2.4 copy-done.11
  270.5 2.3 copy-done.14
  272.8 6.4 %reshape.89 = f32[8,256,640]{2,1,0:T(8,128)} reshape(f32[256,5120]{1,0:T(8,128)} %copy-done.11) | data formatting | bytes 10485760 | tf_op jit(solution)/shard_map/reshape | solution.py:36
  279.2 6.3 %reshape.90 = f32[8,256,640]{2,1,0:T(8,128)} reshape(f32[256,5120]{1,0:T(8,128)} %copy-done.14) | data formatting | bytes 10485760 | tf_op jit(solution)/shard_map/reshape | solution.py:33
  286.5 53.6 %while.61 = (s32[]{:T(128)}, f32[8,640]{1,0:T(8,128)S(1)}, f32[8,640]{1,0:T(8,128)S(1)}, f32[32,8,640]{2,1,0:T(8,128)S(1)}, f32[32,8,640]{2,1,0:T(8,128)}, /*ind...) while((s32[]{:T(128)}, f32[8,640]{1,0:T(8,128)S(1)}, ...), condition=%wide.region_5.6_spmd.clone, body=%wide.region_4.5_spmd.clone.sunk | while | flops 35844 | bytes 286852 | solution.py:51
  341.3 5.0 fusion.21
  346.4 2.4 copy-done.3
  350.7 17.3 %while.59 = (s32[]{:T(128)}, f32[8,640]{1,0:T(8,128)S(1)}, f32[8,640]{1,0:T(8,128)S(1)}, f32[8,640]{1,0:T(8,128)S(1)}, s32[]{:T(128)}) while((s32[]{:T(128)}, f32[8,640]{1,0:T(8,128)S(1)}, f32[8,640]{1,0:T(8,128)S(1)}, f32[8,640]{1,0:T(8,128)S(1)}, s32[]{:T(128)}) %tuple.165), condition=%wide.region_7.8_spmd, body=%wide.region_6.7_spmd.sunk | while | flops 10242 | bytes 163941 | solution.py:102
  350.7 1.3 collective-permute-start.1
  352.0 4.7 collective-permute-done.1
  357.9 4.4 collective-permute-done.1
  363.6 4.4 collective-permute-done.1
  368.0 17.6 %multiply_convert_fusion = (bf16[8,256,640]{2,1,0:T(8,128)(2,1)S(1)}, bf16[8,256,640]{2,1,0:T(8,128)(2,1)}, bf16[8,256,640]{2,1,0:T(8,128)(2,1)}) fusion(f32[8,256,1920]{2,1,0:T(8,128)} %bitcast.104, f32[8,256,640]{2,1,0:T(8,128)} %copy-done.3, f32[8,640]{1,0:T(8,128)S(1)} %get-tuple-element.233, f32[8,256,640]{2,1,0:T(8,128)} %reshape.90, ...), kind=kLoop, calls=%fused_computation.54 | loop fusion | flops 32768000 | bytes 45248512 | tf_op jit(solution)/shard_map/convert
  385.6 1.5 copy-done.6
  387.2 16.0 %convolution_bitcast_fusion = f32[1280,1920]{1,0:T(8,128)} fusion(bf16[8,256,640]{2,1,0:T(8,128)(2,1)} %get-tuple-element.363, bf16[8,256,640]{2,1,0:T(8,128)(2,1)} %get-tuple-element.392, bf16[8,256,640]{2,1,0:T(8,128)(2,1)S(1)} %get-tuple-element.391, bf16[8,256,640]{1,2,0:T(8,128)(2,1)} %copy-done.9, bf16[8,256,640]{1,2,0:T(8,128)(2,1)S(1)} %copy.34), kind=kOutput, calls=%fused_computation.19 | convolution fusion | flops 10100408320 | bytes 22937600 | tf_op jit(solution)/shard_map/dot_general | solution.py:130
  403.1 1.7 copy-done.7
  404.9 16.9 %fusion.23 = f32[8,256,1280]{2,1,0:T(8,128)} fusion(bf16[1280,1920]{1,0:T(8,128)(2,1)} %all-gather.2.cloned.1.call-done, bf16[8,256,640]{2,1,0:T(8,128)(2,1)} %get-tuple-element.363, bf16[8,256,640]{2,1,0:T(8,128)(2,1)} %get-tuple-element.392, bf16[8,256,640]{2,1,0:T(8,128)(2,1)S(1)} %copy-done.7), kind=kOutput, calls=%fused_computation.57 | convolution fusion | flops 10089922560 | bytes 23265280 | tf_op jit(solution)/shard_map/dot_general | solution.py:117
  421.8 3.3 slice_multiply_fusion
  425.1 1.4 collective-permute-start.3
  426.6 1.3 convert_reduce_fusion
  427.9 2.7 slice.232
  430.6 42.3 %psum.7 = f32[1920]{0:T(1024)} all-reduce(f32[1920]{0:T(1024)S(1)} %convert_reduce_fusion), channel_id=1, replica_groups=mesh['seq'=4,'dp'=8] {'seq','dp'}, use_global_device_ids=true, to_apply=%region_10.11 | all-reduce | flops 1920 | bytes 15360 | tf_op jit(solution)/shard_map/psum | solution.py:116
  473.0 6.3 %fusion.7 = bf16[8,256,640]{2,1,0:T(8,128)(2,1)} fusion(f32[8,256,1280]{2,1,0:T(8,128)} %fusion.23, f32[8,1,640]{2,1,0:T(1,128)S(1)} %copy.44, f32[8,255,640]{2,1,0:T(8,128)} %slice.232), kind=kLoop, calls=%fused_computation.29 | loop fusion | flops 3932160 | bytes 13107200 | tf_op jit(solution)/shard_map/convert_element_type | solution.py:127
  479.3 60.8 %reduce-scatter.4.cloned.1.call-done = f32[40,1920]{1,0:T(8,128)} async-done(((f32[1280,1920]{1,0:T(8,128)}), f32[40,1920]{1,0:T(8,128)}) %reduce-scatter.4.cloned.1.call-update) | async-done | bytes 307216
  (278 shorter events, 121.4 us)
Async XLA Ops:
  7.2 70.9 %all-gather.2.cloned.1.call-start = ((), (), s32[]{:S(2)}) async-start(), calls=%async_computation.1 | async-start | bytes 5068800 | tf_op jit(solution)/shard_map/all_gather | solution.py:71
  7.9 532.2 %reduce-scatter.4.cloned.1.call-start = ((), (), s32[]{:S(2)}) async-start(), calls=%async_computation.2 | async-start | bytes 10137600
  8.9 9.4 %collective-permute-start.2 = (bf16[8,640]{1,0:T(8,128)(2,1)S(1)}, bf16[8,640]{1,0:T(8,128)(2,1)S(1)}, u32[]{:S(2)}, u32[]{:S(2)}) collective-permute-start(bf16[8,640]{1,0:T(8,128)(2,1)S(1)} %bitcast.124), channel_id=1, source_target_pairs={{0,8},{8,16},{16,24},{1,9},{9,17},{17,25},{2,10},{10,18},{18,26},{... | collective-permute-start | bytes 30728 | tf_op jit(solution)/shard_map/ppermute | solution.py:12
  22.4 1.5 copy-start.9
  26.6 51.4 %copy-start.16 = (f32[1920]{0:T(1024)S(1)}, f32[1920]{0:T(1024)}, u32[]{:S(2)}) copy-start(f32[1920]{0:T(1024)} %param.15) | copy-start | bytes 23044
  92.4 8.5 %copy-start.1 = (f32[2048,1920]{1,0:T(8,128)}, f32[2048,1920]{1,0:T(8,128)S(1)}, u32[]{:S(2)}) copy-start(f32[2048,1920]{1,0:T(8,128)S(1)} %broadcast_add_fusion) | copy-start | bytes 47185924
  118.9 6.2 %slice-start = ((s8[5242880]{0:T(1024)(128)(4,1)}), s8[4194304]{0:T(1024)(128)(4,1)S(1)}, s32[]{:S(2)}) async-start(s8[5242880]{0:T(1024)(128)(4,1)} %bitcast.106), calls=%async_computation.3 | async-start | bytes 8388608
  120.5 4.6 copy-start.2
  120.5 4.6 slice-start.1
  127.7 2.3 copy-start.12
  130.1 2.4 copy-start.13
  187.0 0.8 copy-start.15
  208.6 2.3 copy-start.4
  208.6 4.0 copy-start.5
  212.7 5.3 collective-permute-start
  218.0 5.7 %collective-permute-start = (f32[8,640]{1,0:T(8,128)S(1)}, f32[8,640]{1,0:T(8,128)S(1)}, u32[]{:S(2)}, u32[]{:S(2)}) collective-permute-start(f32[8,640]{1,0:T(8,128)S(1)} %multiply_add_fusion.6), channel_id=1, source_target_pairs={{0,8},{8,16},{16,24},{1,9},{9,17},{17,25},{2,10},{10,18},{18,26},{... | collective-permute-start | bytes 61448 | tf_op jit(solution)/shard_map/while/body/eval_jaxpr/ppermute | solution.py:12
  223.7 5.7 %collective-permute-start = (f32[8,640]{1,0:T(8,128)S(1)}, f32[8,640]{1,0:T(8,128)S(1)}, u32[]{:S(2)}, u32[]{:S(2)}) collective-permute-start(f32[8,640]{1,0:T(8,128)S(1)} %multiply_add_fusion.6), channel_id=1, source_target_pairs={{0,8},{8,16},{16,24},{1,9},{9,17},{17,25},{2,10},{10,18},{18,26},{... | collective-permute-start | bytes 61448 | tf_op jit(solution)/shard_map/while/body/eval_jaxpr/ppermute | solution.py:12
  258.4 4.3 copy-start
  258.4 8.5 %slice-start.2 = ((s8[5242880]{0:T(1024)(128)(4,1)}), s8[4194304]{0:T(1024)(128)(4,1)S(1)}, s32[]{:S(2)}) async-start(s8[5242880]{0:T(1024)(128)(4,1)} %bitcast.108), calls=%async_computation.5 | async-start | bytes 8388608
  262.7 4.2 slice-start.3
  268.1 2.4 copy-start.11
  270.5 2.3 copy-start.14
  346.4 2.4 copy-start.3
  350.7 6.0 %collective-permute-start.1 = (f32[8,640]{1,0:T(8,128)S(1)}, f32[8,640]{1,0:T(8,128)S(1)}, u32[]{:S(2)}, u32[]{:S(2)}) collective-permute-start(f32[8,640]{1,0:T(8,128)S(1)} %multiply_add_fusion.7), channel_id=1, source_target_pairs={{8,0},{16,8},{24,16},{9,1},{17,9},{25,17},{10,2},{18,10},{26,18},{... | collective-permute-start | bytes 61448 | tf_op jit(solution)/shard_map/while/body/eval_jaxpr/ppermute | solution.py:12
  356.6 5.7 %collective-permute-start.1 = (f32[8,640]{1,0:T(8,128)S(1)}, f32[8,640]{1,0:T(8,128)S(1)}, u32[]{:S(2)}, u32[]{:S(2)}) collective-permute-start(f32[8,640]{1,0:T(8,128)S(1)} %multiply_add_fusion.7), channel_id=1, source_target_pairs={{8,0},{16,8},{24,16},{9,1},{17,9},{25,17},{10,2},{18,10},{26,18},{... | collective-permute-start | bytes 61448 | tf_op jit(solution)/shard_map/while/body/eval_jaxpr/ppermute | solution.py:12
  362.3 5.7 %collective-permute-start.1 = (f32[8,640]{1,0:T(8,128)S(1)}, f32[8,640]{1,0:T(8,128)S(1)}, u32[]{:S(2)}, u32[]{:S(2)}) collective-permute-start(f32[8,640]{1,0:T(8,128)S(1)} %multiply_add_fusion.7), channel_id=1, source_target_pairs={{8,0},{16,8},{24,16},{9,1},{17,9},{25,17},{10,2},{18,10},{26,18},{... | collective-permute-start | bytes 61448 | tf_op jit(solution)/shard_map/while/body/eval_jaxpr/ppermute | solution.py:12
  385.6 1.5 copy-start.6
  403.1 1.7 copy-start.7
  421.8 4.8 copy-start.8
  421.8 4.8 copy-start.10
  425.1 47.9 %collective-permute-start.3 = (f32[8,640]{1,0:T(8,128)S(1)}, f32[8,640]{1,0:T(8,128)S(1)}, u32[]{:S(2)}, u32[]{:S(2)}) collective-permute-start(f32[8,640]{1,0:T(8,128)S(1)} %bitcast.121), channel_id=1, source_target_pairs={{8,0},{16,8},{24,16},{9,1},{17,9},{25,17},{10,2},{18,10},{26,18},{... | collective-permute-start | bytes 61448 | tf_op jit(solution)/shard_map/ppermute | solution.py:12
Sparse Core Ops, SparseCore 0:
  10.9 67.0 all-gather.1
  403.3 136.8 reduce-scatter.3
where the time goes:
time: 550 us; the launch traced here: 547 us
  local copies, waits for them, and re-layouts  176 us (32%)
  waiting for transfers between devices  123 us (22%)
  other arithmetic  120 us (22%)
  matrix products  47.3 us (9%)
  blocking collectives  42.3 us (8%)
  starting transfers between devices  22.5 us (4%)
  between operations  14.5 us (3%)
    dynamic_slice x64, local copies, waits for them, and re-layouts, chain_pool(): lax.scan(advance, start, (total_gain, total_state), reverse=reverse)  65.6 us
    unnamed x3, waiting for transfers between devices  61.5 us
    all_gather x1, waiting for transfers between devices, per_device(): lax.all_gather(weights, ('seq', 'dp'), axis=0, tiled=True)  43.5 us
    psum x1, blocking collectives, per_device(): lax.psum(jnp.sum(grad_pre, axis=0, dtype=jnp.float32), ('seq', 'dp'))  42.3 us
    dynamic_update_slice x64, other arithmetic, chain_pool(): lax.scan(advance, start, (total_gain, total_state), reverse=reverse)  39 us
    another operation x2, other arithmetic  28.9 us
    unnamed x52, local copies, waits for them, and re-layouts  28.2 us
    ppermute x8, starting transfers between devices, from_behind(): return lax.ppermute(shard, axis, pairs)  22.4 us
  transfers between devices with their start and end apart: 10, of which 8 were waited for; matrix products, arithmetic and copies ran while one was open for 9% of the time, Pallas kernels for 0%

commit v1 on v0

v1 whole, which is shorter than its diff:
```python
import functools

import jax
import jax.numpy as jnp
from jax import lax
from jax.experimental import pallas as pl
from jax.experimental.pallas import tpu as pltpu
from jax.sharding import PartitionSpec as P

MESH = pl.DeviceIdType.MESH
BF = jnp.bfloat16
F32 = jnp.float32
LANES = 128
STEPS = 32
TWO = 16


def cut_chunks(width):
    tiles = width // LANES
    chunks, at = [], 0
    if tiles % 2:
        chunks.append((0, LANES))
        at = LANES
    while at < width:
        chunks.append((at, 2 * LANES))
        at += 2 * LANES
    return chunks


def dot(a, b):
    return jnp.dot(a, b, preferred_element_type=F32)


def layer_kernel(
    span, chunks,
    tok, wts, bias, resets, up,
    hid, gtok, gw, gb,
    raw_t, raw_u, joined, upt, wv, gates, qf, gp, keepb, perm, pinv, hb, gwv, summ, edge,
    in_sem, w_sem, out_sem, gw_sem, sum_send, sum_recv, edge_send, edge_recv,
):
    seqs, steps, width = tok.shape
    rows = seqs * steps
    block = seqs * STEPS
    blocks = steps // STEPS
    me = lax.axis_index("seq")
    col = lax.axis_index("dp")

    barrier = pltpu.get_barrier_semaphore()
    for k in range(1, span):
        pl.semaphore_signal(
            barrier, inc=1, device_id=(lax.rem(me + k, span), col), device_id_type=MESH
        )
    pl.semaphore_wait(barrier, span - 1)

    in_t = pltpu.make_async_copy(tok, raw_t, in_sem.at[0])
    in_u = pltpu.make_async_copy(up, raw_u, in_sem.at[1])
    in_t.start()
    in_u.start()
    w_copies = []
    for c, (at, cw) in enumerate(chunks):
        for g in range(3):
            w_copies.append(
                pltpu.make_async_copy(
                    wts.at[:, pl.ds(g * width + at, cw)],
                    wv.at[:, pl.ds(3 * at + g * cw, cw)],
                    w_sem.at[c, g],
                )
            )
    for copy in w_copies:
        copy.start()

    r = lax.broadcasted_iota(jnp.int32, (block, block), 0)
    q = lax.broadcasted_iota(jnp.int32, (block, block), 1)
    perm[...] = (((q & 31) == (r >> 3)) & ((q >> 5) == (r & 7))).astype(F32).astype(BF)
    pinv[...] = (((r & 31) == (q >> 3)) & ((r >> 5) == (q & 7))).astype(F32).astype(BF)
    keep = 1.0 - resets[...].astype(F32)
    tiled = jnp.broadcast_to(keep[None], (STEPS, seqs, steps)).reshape(block, steps)
    row_t = lax.broadcasted_iota(jnp.int32, (block, steps), 0) >> 3
    lane_t = lax.broadcasted_iota(jnp.int32, (block, steps), 1)
    ones = jnp.ones((steps, LANES), BF)
    for b in range(blocks):
        picked = jnp.where(lane_t == row_t + b * STEPS, tiled, 0.0).astype(BF)
        keepb[b * block : (b + 1) * block, :] = dot(picked, ones)

    def wide_keep(at, count, lanes):
        k = keepb[pl.ds(at, count), :]
        return jnp.concatenate([k] * (lanes // LANES), axis=1)

    in_t.wait()
    last_rows = raw_t[:, steps - STEPS :, :].reshape(block, width)
    edge[0] = dot(perm[block - TWO :, :], last_rows)[TWO - seqs :]
    to_right = pltpu.make_async_remote_copy(
        src_ref=edge.at[0], dst_ref=edge.at[1], send_sem=edge_send.at[0], recv_sem=edge_recv.at[0],
        device_id=(me + 1, col), device_id_type=MESH,
    )

    @pl.when(me < span - 1)
    def _():
        to_right.start()

    @pl.when(me == 0)
    def _():
        edge[1] = jnp.zeros((seqs, width), F32)

    in_u.wait()

    def stage(b, last):
        at = pl.multiple_of(b * block, block)
        src = raw_t[:, pl.ds(pl.multiple_of(b * STEPS, STEPS), STEPS), :].reshape(block, width)
        now = dot(perm[...], src)
        before = jnp.concatenate([last, now[: block - seqs]], axis=0)
        before = before * wide_keep(at, block, width)
        joined[pl.ds(at, block), :width] = now.astype(BF)
        joined[pl.ds(at, block), width:] = before.astype(BF)
        src = raw_u[:, pl.ds(pl.multiple_of(b * STEPS, STEPS), STEPS), :].reshape(block, width)
        upt[pl.ds(at, block), :] = dot(perm[...], src).astype(BF)
        return now[block - seqs :]

    lax.fori_loop(0, blocks, stage, jnp.zeros((seqs, width), F32))

    @pl.when(me > 0)
    def _():
        to_right.wait_recv()

    @pl.when(me < span - 1)
    def _():
        to_right.wait_send()

    first = jnp.concatenate([edge[1], joined[:TWO, :width].astype(F32)[:seqs]], axis=0)
    joined[:TWO, width:] = (first * wide_keep(0, TWO, width)).astype(BF)

    def pass_a(c):
        at, cw = chunks[c]
        base = 3 * at
        size = 2 * block if blocks % 2 == 0 else block
        halves = range(cw // LANES)
        biases = [
            [
                jnp.broadcast_to(
                    bias[0:1, g * width + at + h * LANES : g * width + at + (h + 1) * LANES],
                    (TWO, LANES),
                )
                for h in halves
            ]
            for g in range(3)
        ]
        biases[1] = [0.5 * v for v in biases[1]]
        biases[2] = [0.5 * v for v in biases[2]]

        def body(i, carry):
            carry = [list(v) for v in carry]
            r0 = pl.multiple_of(i * size, size)
            gates[pl.ds(r0, size), base : base + 3 * cw] = dot(
                joined[pl.ds(r0, size), :], wv[:, base : base + 3 * cw]
            )
            for j in range(size // TWO):
                sl = pl.ds(r0 + j * TWO, TWO)
                k = keepb[sl, :]
                for h in halves:
                    zc, fc, oc = (base + g * cw + h * LANES for g in range(3))
                    z = jnp.tanh(gates[sl, zc : zc + LANES] + biases[0][h])
                    f = 0.5 * jnp.tanh(0.5 * gates[sl, fc : fc + LANES] + biases[1][h]) + 0.5
                    o = 0.5 * jnp.tanh(0.5 * gates[sl, oc : oc + LANES] + biases[2][h]) + 0.5
                    gates[sl, zc : zc + LANES] = z
                    gates[sl, fc : fc + LANES] = f
                    gates[sl, oc : oc + LANES] = o
                    g = upt[sl, at + h * LANES : at + (h + 1) * LANES].astype(F32)
                    eff = f * k
                    fresh = (1.0 - f) * z
                    src = g * o
                    gain, state, back = carry[h]
                    for m in (0, seqs):
                        gain = gain * eff[m : m + seqs]
                        state = state * eff[m : m + seqs] + fresh[m : m + seqs]
                        back = back + gain * src[m : m + seqs]
                    carry[h] = [gain, state, back]
            return tuple(tuple(v) for v in carry)

        zero = jnp.zeros((seqs, LANES), F32)
        one = jnp.ones((seqs, LANES), F32)
        done = lax.fori_loop(0, rows // size, body, tuple((one, zero, zero) for _ in halves))
        for h in halves:
            cols = slice(at + h * LANES, at + (h + 1) * LANES)
            for v in range(3):
                summ[me, v * seqs : (v + 1) * seqs, cols] = done[h][v]
        for k in range(1, span):
            exchange(c, k).start()

    def exchange(c, k):
        at, cw = chunks[c]
        here = summ.at[me, :, pl.ds(at, cw)]
        return pltpu.make_async_remote_copy(
            src_ref=here, dst_ref=here, send_sem=sum_send.at[c, k - 1],
            recv_sem=sum_recv.at[c, k - 1],
            device_id=(lax.rem(me + k, span), col), device_id_type=MESH,
        )

    def pass_b(c):
        at, cw = chunks[c]
        base = 3 * at
        halves = range(cw // LANES)
        for k in range(1, span):
            exchange(c, k).wait()
        enter, leave = [], []
        for h in halves:
            cols = slice(at + h * LANES, at + (h + 1) * LANES)
            state = jnp.zeros((seqs, LANES), F32)
            for s in range(span - 1):
                new = summ[s, seqs : 2 * seqs, cols] + summ[s, :seqs, cols] * state
                state = jnp.where(s < me, new, state)
            enter.append(state)
            back = jnp.zeros((seqs, LANES), F32)
            for s in range(span - 1, 0, -1):
                new = summ[s, 2 * seqs :, cols] + summ[s, :seqs, cols] * back
                back = jnp.where(s > me, new, back)
            leave.append(back)

        def forward(i, carry):
            cells, sums = list(carry[0]), list(carry[1])
            r0 = pl.multiple_of(i * block, block)
            for j in range(block // TWO):
                sl = pl.ds(r0 + j * TWO, TWO)
                k = keepb[sl, :]
                for h in halves:
                    zc, fc, oc = (base + g * cw + h * LANES for g in range(3))
                    z = gates[sl, zc : zc + LANES]
                    f = gates[sl, fc : fc + LANES]
                    o = gates[sl, oc : oc + LANES]
                    g = upt[sl, at + h * LANES : at + (h + 1) * LANES].astype(F32)
                    eff = f * k
                    rest = 1.0 - f
                    fresh = rest * z
                    c0 = eff[:seqs] * cells[h] + fresh[:seqs]
                    c1 = eff[seqs:] * c0 + fresh[seqs:]
                    cell = jnp.concatenate([c0, c1], axis=0)
                    prev = jnp.concatenate([cells[h], c0], axis=0)
                    cells[h] = c1
                    hb[j * TWO : (j + 1) * TWO, h * LANES : (h + 1) * LANES] = (o * cell).astype(BF)
                    src = g * o
                    go = src * cell * (1.0 - o)
                    gp[sl, oc : oc + LANES] = go.astype(BF)
                    sums[h] = sums[h] + go
                    gates[sl, zc : zc + LANES] = rest * (1.0 - z * z)
                    gates[sl, fc : fc + LANES] = eff
                    gates[sl, oc : oc + LANES] = src
                    qf[sl, h * LANES : (h + 1) * LANES] = (prev * k - z) * (f * rest)
            out = dot(pinv[...], hb[:, :cw]).astype(BF).reshape(seqs, STEPS, cw)
            raw_t[:, pl.ds(pl.multiple_of(i * STEPS, STEPS), STEPS), at : at + cw] = out
            return tuple(cells), tuple(sums)

        zero = jnp.zeros((TWO, LANES), F32)
        zeros = tuple(zero for _ in halves)
        _, sum_o = lax.fori_loop(0, blocks, forward, (tuple(enter), zeros))

        def backward(n, carry):
            heads, sums_z, sums_f = (list(v) for v in carry)
            r0 = pl.multiple_of((blocks - 1 - n) * block, block)
            for j in range(block // TWO - 1, -1, -1):
                sl = pl.ds(r0 + j * TWO, TWO)
                for h in halves:
                    zc, fc, oc = (base + g * cw + h * LANES for g in range(3))
                    eff = gates[sl, fc : fc + LANES]
                    src = gates[sl, oc : oc + LANES]
                    g1 = src[seqs:] + heads[h]
                    g0 = src[:seqs] + eff[seqs:] * g1
                    heads[h] = eff[:seqs] * g0
                    gc = jnp.concatenate([g0, g1], axis=0)
                    gz = gc * gates[sl, zc : zc + LANES]
                    gf = gc * qf[sl, h * LANES : (h + 1) * LANES]
                    gp[sl, zc : zc + LANES] = gz.astype(BF)
                    gp[sl, fc : fc + LANES] = gf.astype(BF)
                    sums_z[h] = sums_z[h] + gz
                    sums_f[h] = sums_f[h] + gf
            return tuple(heads), tuple(sums_z), tuple(sums_f)

        _, sum_z, sum_f = lax.fori_loop(0, blocks, backward, (tuple(leave), zeros, zeros))
        for h in halves:
            for g, total in enumerate((sum_z, sum_f, sum_o)):
                lane = g * width + at + h * LANES
                gb[0:1, lane : lane + LANES] = jnp.sum(total[h], axis=0, keepdims=True)

    def gw_copies(c):
        at, cw = chunks[c]
        return [
            pltpu.make_async_copy(
                gwv.at[c % 2, :, pl.ds(g * cw, cw)],
                gw.at[:, pl.ds(g * width + at, cw)],
                gw_sem.at[c, g],
            )
            for g in range(3)
        ]

    def pass_c(c):
        at, cw = chunks[c]
        base = 3 * at
        tile = 2 * LANES
        if c >= 2:
            for copy in gw_copies(c - 2):
                copy.wait()

        def body(i, carry):
            r0 = pl.multiple_of(i * tile, tile)
            gwv[c % 2, pl.ds(r0, tile), : 3 * cw] = lax.dot_general(
                joined[:, pl.ds(r0, tile)], gp[:, base : base + 3 * cw],
                (((0,), (0,)), ((), ())), preferred_element_type=F32,
            )
            return carry

        lax.fori_loop(0, 2 * width // tile, body, 0)
        for copy in gw_copies(c):
            copy.start()

    for c in range(len(chunks)):
        for g in range(3):
            w_copies[3 * c + g].wait()
        pass_a(c)
    for c in range(len(chunks)):
        pass_b(c)
        pass_c(c)
    out_h = pltpu.make_async_copy(raw_t, hid, out_sem.at[0])
    out_h.start()

    to_left = pltpu.make_async_remote_copy(
        src_ref=edge.at[2], dst_ref=edge.at[3], send_sem=edge_send.at[1], recv_sem=edge_recv.at[1],
        device_id=(me - 1, col), device_id_type=MESH,
    )

    @pl.when(me == span - 1)
    def _():
        edge[3] = jnp.zeros((seqs, width), F32)

    def put(b):
        at = pl.multiple_of(b * block, block)
        out = dot(pinv[...], gates[pl.ds(at, block), :width].astype(BF)).astype(BF)
        raw_u[:, pl.ds(pl.multiple_of(b * STEPS, STEPS), STEPS), :] = out.reshape(
            seqs, STEPS, width
        )

    def inputs(i, pend):
        r0 = pl.multiple_of(i * block, block)
        both = lax.dot_general(
            gp[pl.ds(r0, block), :], wv[...], (((1,), (1,)), ((), ())), preferred_element_type=F32
        )
        own = both[:, :width]
        late = both[:, width:] * wide_keep(r0, block, width)
        gates[pl.ds(r0, block - seqs), :width] = own[: block - seqs] + late[seqs:]

        @pl.when(i == 0)
        def _():
            edge[2] = late[:seqs]

            @pl.when(me > 0)
            def _():
                to_left.start()

        @pl.when(i > 0)
        def _():
            gates[pl.ds(pl.multiple_of(r0 - seqs, seqs), seqs), :width] = pend + late[:seqs]
            put(i - 1)

        return own[block - seqs :]

    pend = lax.fori_loop(0, blocks, inputs, jnp.zeros((seqs, width), F32))

    @pl.when(me < span - 1)
    def _():
        to_left.wait_recv()

    @pl.when(me > 0)
    def _():
        to_left.wait_send()

    gates[rows - seqs :, :width] = pend + edge[3]
    put(blocks - 1)
    out_t = pltpu.make_async_copy(raw_u, gtok, out_sem.at[1])
    out_t.start()
    for c in range(max(0, len(chunks) - 2), len(chunks)):
        for copy in gw_copies(c):
            copy.wait()
    out_h.wait()
    out_t.wait()


def per_device(tokens, weights, bias, resets, upstream):
    seqs, steps, width = tokens.shape
    rows = seqs * steps
    span = lax.axis_size("seq")
    chunks = cut_chunks(width)
    block = seqs * STEPS
    full = lax.all_gather(weights, ("seq", "dp"), axis=0, tiled=True)
    any_spec = pl.BlockSpec(memory_space=pl.ANY)
    vmem = pl.BlockSpec(memory_space=pltpu.VMEM)
    hid, gtok, gw, gb = pl.pallas_call(
        functools.partial(layer_kernel, span, chunks),
        out_shape=(
            jax.ShapeDtypeStruct(tokens.shape, BF),
            jax.ShapeDtypeStruct(tokens.shape, BF),
            jax.ShapeDtypeStruct((2 * width, 3 * width), F32),
            jax.ShapeDtypeStruct((1, 3 * width), F32),
        ),
        in_specs=[any_spec, any_spec, vmem, vmem, any_spec],
        out_specs=(any_spec, any_spec, any_spec, vmem),
        scratch_shapes=[
            pltpu.VMEM(tokens.shape, BF),
            pltpu.VMEM(tokens.shape, BF),
            pltpu.VMEM((rows, 2 * width), BF),
            pltpu.VMEM((rows, width), BF),
            pltpu.VMEM((2 * width, 3 * width), BF),
            pltpu.VMEM((rows, 3 * width), F32),
            pltpu.VMEM((rows, 2 * LANES), F32),
            pltpu.VMEM((rows, 3 * width), BF),
            pltpu.VMEM((rows, LANES), F32),
            pltpu.VMEM((block, block), BF),
            pltpu.VMEM((block, block), BF),
            pltpu.VMEM((block, 2 * LANES), BF),
            pltpu.VMEM((2, 2 * width, 6 * LANES), F32),
            pltpu.VMEM((span, 3 * seqs, width), F32),
            pltpu.VMEM((4, seqs, width), F32),
            pltpu.SemaphoreType.DMA((2,)),
            pltpu.SemaphoreType.DMA((len(chunks), 3)),
            pltpu.SemaphoreType.DMA((2,)),
            pltpu.SemaphoreType.DMA((len(chunks), 3)),
            pltpu.SemaphoreType.DMA((len(chunks), span - 1)),
            pltpu.SemaphoreType.DMA((len(chunks), span - 1)),
            pltpu.SemaphoreType.DMA((2,)),
            pltpu.SemaphoreType.DMA((2,)),
        ],
        compiler_params=pltpu.CompilerParams(
            collective_id=0, has_side_effects=True, vmem_limit_bytes=60 << 20
        ),
        name="layer",
    )(tokens, full, bias.reshape(1, -1), resets, upstream)
    gw = lax.psum_scatter(gw, ("seq", "dp"), scatter_dimension=0, tiled=True)
    gb = lax.psum(gb[0], ("seq", "dp"))
    return hid, gtok, gw, gb


def solution(mesh):
    spread = P("dp", "seq", None)
    rows = P(("seq", "dp"), None)
    return jax.shard_map(
        per_device,
        mesh=mesh,
        in_specs=(spread, rows, P(), P("dp", "seq"), spread),
        out_specs=(spread, spread, rows, P()),
        check_vma=False,
    )
```

time: 550 us -> 299 us (0.54)
  local copies, waits for them, and re-layouts: 176 us -> 6.96 us
  other arithmetic: 120 us -> 0.02 us
  Pallas kernels: 0 us -> 72.2 us
  matrix products: 47.3 us -> 0 us
  waiting for transfers between devices: 123 us -> 167 us
  starting transfers between devices: 22.5 us -> 0.08 us
    pallas_call x0 -> x1, Pallas kernels: none -> 72.2 us  [per_device(): pl.pallas_call(functools.partial(layer_kernel, span, chunks), out_shape=(...]
    dynamic_slice x64 -> x0, local copies, waits for them, and re-layouts: 65.6 us -> none  [chain_pool(): lax.scan(advance, start, (total_gain, total_state), reverse=reverse)]
    reshape x8 -> x1, local copies, waits for them, and re-layouts: 50.8 us -> 1.3 us  [per_device(): bias.reshape(1, -1)]
    dot_general x3 -> x0, matrix products: 47.3 us -> none  [the longest x1 16.9 us: per_device(): lax.dot_general(grad_pre, lax.all_gather(weights, ('seq', 'dp'), axis=0,...]
    dynamic_update_slice x64 -> x0, other arithmetic: 39 us -> none  [chain_pool(): lax.scan(advance, start, (total_gain, total_state), reverse=reverse)]
    unnamed x3, waiting for transfers between devices: 61.5 us -> 98.4 us
    another operation x2 -> x0, other arithmetic: 28.9 us -> none
    all_gather x1, waiting for transfers between devices: 43.5 us -> 68.8 us  [per_device(): full = lax.all_gather(weights, ('seq', 'dp'), axis=0, tiled=True)]
  transfers between devices with their start and end apart: 10 -> 2, of which waited for: 8 -> 2; matrix products, arithmetic and copies ran while one was open for 9% -> 0% of each run, Pallas kernels for 0% -> 0%
where the time goes in v1:
time: 299 us
  waiting for transfers between devices  167 us (56%)
  Pallas kernels  72.2 us (24%)
  blocking collectives  38.4 us (13%)
  between operations  14.1 us (5%)
  local copies, waits for them, and re-layouts  6.96 us (2%)
    unnamed x3, waiting for transfers between devices  98.4 us
    pallas_call x1, Pallas kernels, per_device(): pl.pallas_call(functools.partial(layer_kernel, span, chunks), out_shape=(...  72.2 us
    all_gather x1, waiting for transfers between devices, per_device(): full = lax.all_gather(weights, ('seq', 'dp'), axis=0, tiled=True)  68.8 us
    psum x1, blocking collectives, per_device(): gb = lax.psum(gb[0], ('seq', 'dp'))  38.4 us
  transfers between devices with their start and end apart: 2, of which 2 were waited for; matrix products, arithmetic and copies ran while one was open for 0% of the time, Pallas kernels for 0%

profile of v1, /device:TPU:0, one launch (start us, length us, event | category | flops | bytes accessed | tf_op | source)
XLA Modules:
  0.0 298.9 jit_solution(16093717731708078802)
XLA Ops:
  7.2 0.0 all-gather.2.cloned.1.call-start
  7.2 0.7 all-gather.2.cloned.1.call-update
  7.9 0.0 reduce-scatter.4.cloned.1.call-start
  7.9 1.3 reshape.11.bias
  9.2 68.8 %all-gather.2.cloned.1.call-done.wts = bf16[1280,1920]{1,0:T(8,128)(2,1)} async-done(((bf16[40,1920]{1,0:T(8,128)(2,1)}), bf16[1280,1920]{1,0:T(8,128)(2,1)}) %all-gather.2.cloned.1.call-update) | async-done | bytes 4915216 | tf_op jit(solution)/shard_map/all_gather | solution.py:390
  78.0 72.2 %layer.1 = (bf16[8,256,640]{2,1,0:T(8,128)(2,1)}, bf16[8,256,640]{2,1,0:T(8,128)(2,1)}, f32[1280,1920]{1,0:T(8,128)}, f32[1,1920]{1,0:T(1,128)}) custom-call(bf16[8,256,640]{2,1,0:T(8,128)(2,1)} %tok.1, bf16[1280,1920]{1,0:T(8,128)(2,1)} %all-gather.2.cloned.1.call-done.wts, f32[1,1920]{1,0:T(1,128)} %reshape.11.bias, s32[8,256]{1,0:T(8,128)} %resets.1, ...), custom_call_target="tpu_custom_call" | custom-call | tf_op jit(solution)/shard_map/layer/pallas_call | solution.py:393
  150.2 0.0 copy-start.1
  150.2 0.0 reduce-scatter.4.cloned.1.call-update
  150.3 0.7 copy-done.1
  151.0 38.4 %psum.7 = f32[1920]{0:T(1024)} all-reduce(f32[1920]{0:T(1024)S(1)} %reduce), channel_id=1, replica_groups=mesh['seq'=4,'dp'=8] {'seq','dp'}, use_global_device_ids=true, to_apply=%region_1.0 | all-reduce | flops 1920 | bytes 15360 | tf_op jit(solution)/shard_map/psum | solution.py:434
  189.3 0.0 copy-start
  189.3 97.7 %reduce-scatter.4.cloned.1.call-done = f32[40,1920]{1,0:T(8,128)} async-done(((f32[1280,1920]{1,0:T(8,128)}), f32[40,1920]{1,0:T(8,128)}) %reduce-scatter.4.cloned.1.call-update) | async-done | bytes 307216
  287.0 3.5 %copy.11 = bf16[8,256,640]{2,1,0:T(8,128)(2,1)} copy(bf16[8,256,640]{2,1,0:T(8,128)(2,1)} %get-tuple-element.16) | data formatting | bytes 5242880
  290.5 0.0 copy-done
  290.5 1.5 copy.12
  (1 shorter events, 0.0 us)
Async XLA Ops:
  7.2 70.9 %all-gather.2.cloned.1.call-start = ((), (), s32[]{:S(2)}) async-start(), calls=%async_computation.1 | async-start | bytes 5068800 | tf_op jit(solution)/shard_map/all_gather | solution.py:390
  7.9 279.1 %reduce-scatter.4.cloned.1.call-start = ((), (), s32[]{:S(2)}) async-start(), calls=%async_computation.2 | async-start | bytes 10137600
  150.2 0.7 copy-start.1
  189.3 101.2 %copy-start = (bf16[8,256,640]{2,1,0:T(8,128)(2,1)S(1)}, bf16[8,256,640]{2,1,0:T(8,128)(2,1)}, u32[]{:S(2)}) copy-start(bf16[8,256,640]{2,1,0:T(8,128)(2,1)} %get-tuple-element.17) | copy-start | bytes 7864324
Sparse Core Ops, SparseCore 0:
  10.9 67.0 all-gather.1
  150.4 136.5 reduce-scatter.3

commit v2 on v1

v2 whole, which is shorter than its diff:
```python
import functools

import jax
import jax.numpy as jnp
from jax import lax
from jax.experimental import pallas as pl
from jax.experimental.pallas import tpu as pltpu
from jax.sharding import PartitionSpec as P

MESH = pl.DeviceIdType.MESH
BF = jnp.bfloat16
F32 = jnp.float32
LANES = 128
TRIO = 3 * LANES
STEPS = 32
TWO = 16


def cut_chunks(width):
    tiles = width // LANES
    chunks, at = [], 0
    if tiles % 2:
        chunks.append((0, LANES))
        at = LANES
    while at < width:
        chunks.append((at, 2 * LANES))
        at += 2 * LANES
    return chunks


def dot(a, b):
    return jnp.dot(a, b, preferred_element_type=F32)


def dot_rows(a, b):
    return lax.dot_general(a, b, (((0,), (0,)), ((), ())), preferred_element_type=F32)


def dot_columns(a, b):
    return lax.dot_general(a, b, (((1,), (1,)), ((), ())), preferred_element_type=F32)


def layer_kernel(
    span, peers, fused, chunks,
    tok, wts, bias, resets, up,
    hid, gtok, gw, gb,
    raw_t, raw_u, joined, upt, wv, gates, qf, gp, keepb, perm, pinv, hb, cbuf, summ, edge,
    in_sem, w_sem, out_sem, sum_send, sum_recv, edge_send, edge_recv,
    *links,
):
    seqs, steps, width = tok.shape
    rows = seqs * steps
    block = seqs * STEPS
    blocks = steps // STEPS
    depth = 2 * width
    half_rows = depth // 2
    n_chunks = len(chunks)
    me = lax.axis_index("seq")
    col = lax.axis_index("dp")
    core = col & 1
    place = col >> 1
    plane = peers // 2
    slab = depth // (span * plane)
    shard = slab // 2
    over = -(-shard // 16) * 16
    partner = (me, col ^ 1)
    if fused:
        (
            own16, pair, sb1, rb1, rb2, own2, rb3, fin, fin_rx, gbs,
            a0_sem, a1_send, a1_recv, a2_send, a2_recv, a3_sem,
            r1_send, r1_recv, r2_send, r2_recv, r3_send, r3_recv, r4_sem, gb_send, gb_recv,
        ) = links

    def remote(src, dst, send, recv, to):
        return pltpu.make_async_remote_copy(
            src_ref=src, dst_ref=dst, send_sem=send, recv_sem=recv,
            device_id=to, device_id_type=MESH,
        )

    def mult(v, m):
        return pl.multiple_of(v, m)

    in_t = pltpu.make_async_copy(tok, raw_t, in_sem.at[0])
    in_u = pltpu.make_async_copy(up, raw_u, in_sem.at[1])
    if fused:
        in_w = pltpu.make_async_copy(wts, own16, w_sem.at[0])
        in_w.start()
    in_t.start()
    in_u.start()

    barrier = pltpu.get_barrier_semaphore()
    friends = [(lax.rem(me + k, span), col) for k in range(1, span)]
    if fused:
        friends += [(me, col ^ (2 * y)) for y in range(1, plane)] + [partner]
    for friend in friends:
        pl.semaphore_signal(barrier, inc=1, device_id=friend, device_id_type=MESH)
    pl.semaphore_wait(barrier, len(friends))

    def carried(c, who):
        at, cw = chunks[c]
        if cw == LANES:
            return over, mult((slab - over) * who, 16), 3 * at
        return slab, 0, mult(3 * at + TRIO * who, LANES)

    def part(c, who, planes, places):
        count, r0, c0 = carried(c, who)
        return wv.at[planes, places, pl.ds(r0, count), pl.ds(c0, TRIO)]

    def a1(c, x):
        here = part(c, core, me, place)
        return remote(here, here, a1_send.at[c, x - 1], a1_recv.at[c, x - 1], (me ^ x, col))

    def a2(c, y):
        here = part(c, core, slice(None), place)
        return remote(here, here, a2_send.at[c, y - 1], a2_recv.at[c, y - 1], (me, col ^ (2 * y)))

    def a3(c):
        if chunks[c][1] == LANES:
            here = wv.at[
                :, :, pl.ds(mult(over * core, 16), slab - over), pl.ds(3 * chunks[c][0], TRIO)
            ]
        else:
            here = part(c, core, slice(None), slice(None))
        return remote(here, here, a3_sem.at[c, 0], a3_sem.at[c, 1], partner)

    def w_copies(c):
        at, cw = chunks[c]
        return [
            pltpu.make_async_copy(
                wts.at[:, pl.ds(g * width + at + h * LANES, LANES)],
                wv.at[:, pl.ds(3 * at + h * TRIO + g * LANES, LANES)],
                w_sem.at[c, g, h],
            )
            for g in range(3)
            for h in range(cw // LANES)
        ]

    if fused:
        in_w.wait()
        pair[core] = own16[...].astype(F32)
        a0 = remote(pair.at[core], pair.at[core], a0_sem.at[0], a0_sem.at[1], partner)
        a0.start()
    else:
        for c in range(n_chunks):
            for copy in w_copies(c):
                copy.start()

    r = lax.broadcasted_iota(jnp.int32, (block, block), 0)
    q = lax.broadcasted_iota(jnp.int32, (block, block), 1)
    perm[...] = (((q & 31) == (r >> 3)) & ((q >> 5) == (r & 7))).astype(F32).astype(BF)
    pinv[...] = (((r & 31) == (q >> 3)) & ((r >> 5) == (q & 7))).astype(F32).astype(BF)

    if fused:
        a0.wait_recv()
        for c, (at, cw) in enumerate(chunks):
            count, top, left = carried(c, core)
            for g in range(3):
                lane = g * width + at + (0 if cw == LANES else core * LANES)
                lanes = pl.ds(mult(lane, LANES), LANES)
                both = jnp.concatenate([pair[0, :, lanes], pair[1, :, lanes]], axis=0)
                if count < slab:
                    both = jnp.where(core == 0, both[:count], both[slab - count :])
                to = pl.ds(mult(left + g * LANES, LANES), LANES)
                wv[me, place, pl.ds(top, count), to] = both.astype(BF)
            for x in range(1, span):
                a1(c, x).start()

    keep = 1.0 - resets[...].astype(F32)
    tiled = jnp.broadcast_to(keep[None], (STEPS, seqs, steps)).reshape(block, steps)
    row_t = lax.broadcasted_iota(jnp.int32, (block, steps), 0) >> 3
    lane_t = lax.broadcasted_iota(jnp.int32, (block, steps), 1)
    ones = jnp.ones((steps, LANES), BF)
    for b in range(blocks):
        picked = jnp.where(lane_t == row_t + b * STEPS, tiled, 0.0).astype(BF)
        keepb[b * block : (b + 1) * block, :] = dot(picked, ones)

    def wide_keep(at, count, lanes):
        k = keepb[pl.ds(at, count), :]
        return jnp.concatenate([k] * (lanes // LANES), axis=1)

    in_t.wait()
    last_rows = raw_t[:, steps - STEPS :, :].reshape(block, width)
    edge[0] = dot(perm[block - TWO :, :], last_rows)[TWO - seqs :]
    to_right = remote(edge.at[0], edge.at[1], edge_send.at[0], edge_recv.at[0], (me + 1, col))

    @pl.when(me < span - 1)
    def _():
        to_right.start()

    @pl.when(me == 0)
    def _():
        edge[1] = jnp.zeros((seqs, width), F32)

    in_u.wait()
    if fused:
        for x in range(1, span):
            a1(0, x).wait_recv()
        for y in range(1, plane):
            a2(0, y).start()

    def stage(b, last):
        at = mult(b * block, block)
        src = raw_t[:, pl.ds(mult(b * STEPS, STEPS), STEPS), :].reshape(block, width)
        now = dot(perm[...], src)
        before = jnp.concatenate([last, now[: block - seqs]], axis=0)
        before = before * wide_keep(at, block, width)
        joined[pl.ds(at, block), :width] = now.astype(BF)
        joined[pl.ds(at, block), width:] = before.astype(BF)
        src = raw_u[:, pl.ds(mult(b * STEPS, STEPS), STEPS), :].reshape(block, width)
        upt[pl.ds(at, block), :] = dot(perm[...], src).astype(BF)
        return now[block - seqs :]

    lax.fori_loop(0, blocks, stage, jnp.zeros((seqs, width), F32))

    @pl.when(me > 0)
    def _():
        to_right.wait_recv()

    @pl.when(me < span - 1)
    def _():
        to_right.wait_send()

    first = jnp.concatenate([edge[1], joined[:TWO, :width].astype(F32)[:seqs]], axis=0)
    joined[:TWO, width:] = (first * wide_keep(0, TWO, width)).astype(BF)

    def weights_of(base, count):
        if fused:
            return wv[:, :, :, base : base + count].reshape(depth, count)
        return wv[:, base : base + count]

    def pass_a(c):
        at, cw = chunks[c]
        base = 3 * at
        size = 2 * block if blocks % 2 == 0 else block
        halves = range(cw // LANES)

        def bias_rows(g, h):
            lane = g * width + at + h * LANES
            return jnp.broadcast_to(bias[0:1, lane : lane + LANES], (TWO, LANES))

        bias_z = [bias_rows(0, h) for h in halves]
        bias_f = [0.5 * bias_rows(1, h) for h in halves]
        bias_o = [0.5 * bias_rows(2, h) for h in halves]

        def body(i, carry):
            carry = [list(v) for v in carry]
            r0 = mult(i * size, size)
            gates[pl.ds(r0, size), base : base + 3 * cw] = dot(
                joined[pl.ds(r0, size), :], weights_of(base, 3 * cw)
            )
            for j in range(size // TWO):
                sl = pl.ds(r0 + j * TWO, TWO)
                k = keepb[sl, :]
                for h in halves:
                    zc, fc, oc = (base + h * TRIO + g * LANES for g in range(3))
                    z = jnp.tanh(gates[sl, zc : zc + LANES] + bias_z[h])
                    f = 0.5 * jnp.tanh(0.5 * gates[sl, fc : fc + LANES] + bias_f[h]) + 0.5
                    o = 0.5 * jnp.tanh(0.5 * gates[sl, oc : oc + LANES] + bias_o[h]) + 0.5
                    gates[sl, zc : zc + LANES] = z
                    gates[sl, fc : fc + LANES] = f
                    gates[sl, oc : oc + LANES] = o
                    g = upt[sl, at + h * LANES : at + (h + 1) * LANES].astype(F32)
                    eff = f * k
                    fresh = (1.0 - f) * z
                    src = g * o
                    gain, state, back = carry[h]
                    for m in (0, seqs):
                        gain = gain * eff[m : m + seqs]
                        state = state * eff[m : m + seqs] + fresh[m : m + seqs]
                        back = back + gain * src[m : m + seqs]
                    carry[h] = [gain, state, back]
            return tuple(tuple(v) for v in carry)

        zero = jnp.zeros((seqs, LANES), F32)
        one = jnp.ones((seqs, LANES), F32)
        done = lax.fori_loop(0, rows // size, body, tuple((one, zero, zero) for _ in halves))
        for h in halves:
            cols = slice(at + h * LANES, at + (h + 1) * LANES)
            for v in range(3):
                summ[me, v * seqs : (v + 1) * seqs, cols] = done[h][v]
        for k in range(1, span):
            exchange(c, k).start()

    def exchange(c, k):
        at, cw = chunks[c]
        here = summ.at[me, :, pl.ds(at, cw)]
        return remote(
            here, here, sum_send.at[c, k - 1], sum_recv.at[c, k - 1], (lax.rem(me + k, span), col)
        )

    def pass_b(c):
        at, cw = chunks[c]
        base = 3 * at
        halves = range(cw // LANES)
        for k in range(1, span):
            exchange(c, k).wait()
        enter, leave = [], []
        for h in halves:
            cols = slice(at + h * LANES, at + (h + 1) * LANES)
            state = jnp.zeros((seqs, LANES), F32)
            for s in range(span - 1):
                new = summ[s, seqs : 2 * seqs, cols] + summ[s, :seqs, cols] * state
                state = jnp.where(s < me, new, state)
            enter.append(state)
            back = jnp.zeros((seqs, LANES), F32)
            for s in range(span - 1, 0, -1):
                new = summ[s, 2 * seqs :, cols] + summ[s, :seqs, cols] * back
                back = jnp.where(s > me, new, back)
            leave.append(back)

        def forward(i, carry):
            cells, sums = list(carry[0]), list(carry[1])
            r0 = mult(i * block, block)
            for j in range(block // TWO):
                sl = pl.ds(r0 + j * TWO, TWO)
                k = keepb[sl, :]
                for h in halves:
                    zc, fc, oc = (base + h * TRIO + g * LANES for g in range(3))
                    z = gates[sl, zc : zc + LANES]
                    f = gates[sl, fc : fc + LANES]
                    o = gates[sl, oc : oc + LANES]
                    g = upt[sl, at + h * LANES : at + (h + 1) * LANES].astype(F32)
                    eff = f * k
                    rest = 1.0 - f
                    fresh = rest * z
                    c0 = eff[:seqs] * cells[h] + fresh[:seqs]
                    c1 = eff[seqs:] * c0 + fresh[seqs:]
                    cell = jnp.concatenate([c0, c1], axis=0)
                    prev = jnp.concatenate([cells[h], c0], axis=0)
                    cells[h] = c1
                    hb[j * TWO : (j + 1) * TWO, h * LANES : (h + 1) * LANES] = (o * cell).astype(BF)
                    src = g * o
                    go = src * cell * (1.0 - o)
                    gp[sl, oc : oc + LANES] = go.astype(BF)
                    sums[h] = sums[h] + go
                    gates[sl, zc : zc + LANES] = rest * (1.0 - z * z)
                    gates[sl, fc : fc + LANES] = eff
                    gates[sl, oc : oc + LANES] = src
                    qf[sl, h * LANES : (h + 1) * LANES] = (prev * k - z) * (f * rest)
            out = dot(pinv[...], hb[:, :cw]).astype(BF).reshape(seqs, STEPS, cw)
            raw_t[:, pl.ds(mult(i * STEPS, STEPS), STEPS), at : at + cw] = out
            return tuple(cells), tuple(sums)

        zero = jnp.zeros((TWO, LANES), F32)
        zeros = tuple(zero for _ in halves)
        _, sum_o = lax.fori_loop(0, blocks, forward, (tuple(enter), zeros))

        def backward(n, carry):
            heads, sums_z, sums_f = (list(v) for v in carry)
            r0 = mult((blocks - 1 - n) * block, block)
            for j in range(block // TWO - 1, -1, -1):
                sl = pl.ds(r0 + j * TWO, TWO)
                for h in halves:
                    zc, fc, oc = (base + h * TRIO + g * LANES for g in range(3))
                    eff = gates[sl, fc : fc + LANES]
                    src = gates[sl, oc : oc + LANES]
                    g1 = src[seqs:] + heads[h]
                    g0 = src[:seqs] + eff[seqs:] * g1
                    heads[h] = eff[:seqs] * g0
                    gc = jnp.concatenate([g0, g1], axis=0)
                    gz = gc * gates[sl, zc : zc + LANES]
                    gf = gc * qf[sl, h * LANES : (h + 1) * LANES]
                    gp[sl, zc : zc + LANES] = gz.astype(BF)
                    gp[sl, fc : fc + LANES] = gf.astype(BF)
                    sums_z[h] = sums_z[h] + gz
                    sums_f[h] = sums_f[h] + gf
            return tuple(heads), tuple(sums_z), tuple(sums_f)

        _, sum_z, sum_f = lax.fori_loop(0, blocks, backward, (tuple(leave), zeros, zeros))
        for h in halves:
            for g, total in enumerate((sum_z, sum_f, sum_o)):
                line = jnp.sum(total[h], axis=0, keepdims=True)
                if fused:
                    tile = g * (width // LANES) + at // LANES + h
                    gbs[0, tile : tile + 1, :] = line
                else:
                    lane = g * width + at + h * LANES
                    gb[0:1, lane : lane + LANES] = line

    def gw_copies(c, turn):
        at, cw = chunks[c]
        return [
            pltpu.make_async_copy(
                cbuf.at[turn, :, pl.ds(h * TRIO + g * LANES, LANES)],
                gw.at[pl.ds(turn * half_rows, half_rows), pl.ds(g * width + at + h * LANES, LANES)],
                w_sem.at[c, g, h],
            )
            for g in range(3)
            for h in range(cw // LANES)
        ]

    def pass_c(c, turn):
        at, cw = chunks[c]
        base = 3 * at
        if fused:
            r0 = mult(((me // (span // 2)) ^ 1 ^ turn) * half_rows, LANES)
            result = dot_rows(joined[:, pl.ds(r0, half_rows)], gp[:, base : base + 3 * cw])
            cbuf[turn, :, :, : 3 * cw] = result.reshape(-1, slab, 3 * cw)
            r1(c, turn)
        else:
            if c:
                for copy in gw_copies(c - 1, turn):
                    copy.wait()
            cbuf[turn, :, : 3 * cw] = dot_rows(
                joined[:, turn * half_rows : (turn + 1) * half_rows], gp[:, base : base + 3 * cw]
            )
            for copy in gw_copies(c, turn):
                copy.start()

    def own_part(c, who):
        count, r0, _ = carried(c, who)
        c0 = 0 if chunks[c][1] == LANES else mult(TRIO * who, LANES)
        return pl.ds(r0, count), pl.ds(c0, TRIO)

    def part_rows(c):
        return pl.ds(0, carried(c, 0)[0])

    def orders(turn):
        half = span // 2
        return list(range(half, span)) if turn == 0 else list(range(half - 1, -1, -1))

    def r1_copy(c, turn):
        k = part_rows(c)
        return remote(
            sb1.at[turn, :, k], rb1.at[c, turn, :, k], r1_send.at[c, turn], r1_recv.at[c, turn],
            partner,
        )

    def r1(c, turn):
        if c:
            r1_copy(c - 1, turn).wait_send()
        rs, cs = own_part(c, 1 - core)
        sb1[turn, :, part_rows(c), :] = cbuf[turn, :, rs, cs].astype(BF)
        r1_copy(c, turn).start()

    def r2_copy(c, turn, n, y):
        k = part_rows(c)
        x = orders(turn)[n]
        index = ((me ^ x) % (span // 2)) * plane + (place ^ y)
        return remote(
            rb1.at[c, turn, index, k], rb2.at[c, turn, n, y - 1, k],
            r2_send.at[c, turn, n, y - 1], r2_recv.at[c, turn, n, y - 1], (me, col ^ (2 * y)),
        )

    def r2(c, turn):
        r1_copy(c, turn).wait_recv()
        k = part_rows(c)
        rs, cs = own_part(c, core)
        for n, x in enumerate(orders(turn)):
            for y in range(plane - 1, -1, -1):
                index = ((me ^ x) % (span // 2)) * plane + (place ^ y)
                total = cbuf[turn, index, rs, cs] + rb1[c, turn, index, k].astype(F32)
                if y:
                    rb1[c, turn, index, k] = total.astype(BF)
                    r2_copy(c, turn, n, y).start()
                else:
                    own2[c, turn, n, k] = total

    def r3_copy(c, turn, n):
        k = part_rows(c)
        x = orders(turn)[n]
        return remote(
            rb2.at[c, turn, n, 0, k], rb3.at[c, x - 1, k], r3_send.at[c, x - 1],
            r3_recv.at[c, x - 1], (me ^ x, col),
        )

    def r3(c, turn):
        k = part_rows(c)
        for n, x in enumerate(orders(turn)):
            total = own2[c, turn, n, k]
            for y in range(1, plane):
                r2_copy(c, turn, n, y).wait_recv()
                total = total + rb2[c, turn, n, y - 1, k].astype(F32)
            if x:
                rb2[c, turn, n, 0, k] = total.astype(BF)
                r3_copy(c, turn, n).start()
            else:
                own2[c, turn, n, k] = total

    def r4_copy(c):
        return remote(
            fin.at[c, pl.ds(mult(shard * (1 - core), 8), shard)], fin_rx.at[c],
            r4_sem.at[c, 0], r4_sem.at[c, 1], partner,
        )

    def put_gw(c, tile, value):
        at, cw = chunks[c]
        for g in range(3):
            lane = mult(g * width + at + tile * LANES, LANES)
            gw[:, pl.ds(lane, LANES)] = value[:, g * LANES : (g + 1) * LANES]

    def each_seq_peer(c):
        return [(turn, n, x) for turn in (0, 1) for n, x in enumerate(orders(turn)) if x]

    def r4(c):
        k = part_rows(c)
        total = own2[c, 1, span // 2 - 1, k]
        for turn, n, x in each_seq_peer(c):
            r3_copy(c, turn, n).wait_recv()
            total = total + rb3[c, x - 1, k].astype(F32)
        fin[c, k] = total
        if chunks[c][1] == LANES:
            off = (slab - over) * core
            put_gw(c, 0, fin[c, pl.ds(mult(shard * core - off, 8), shard)])
        else:
            r4_copy(c).start()
            put_gw(c, core, fin[c, pl.ds(mult(shard * core, 8), shard)])

    def r5(c):
        if chunks[c][1] != LANES:
            r4_copy(c).wait_recv()
            put_gw(c, 1 - core, fin_rx[c])

    def gb_stage(stage):
        if stage == 0:
            peer = [((me ^ x, col), x - 1) for x in range(1, span)]
        elif stage == 1:
            peer = [((me, col ^ (2 * y)), span - 1 + y - 1) for y in range(1, plane)]
        else:
            peer = [(partner, span + plane - 2)]
        src = gbs.at[stage]
        return [(remote(src, gbs.at[4 + k], gb_send.at[k], gb_recv.at[k], to), k) for to, k in peer]

    def gb_go(stage):
        for copy, _ in gb_stage(stage):
            copy.start()

    def gb_sum(stage):
        total = gbs[stage]
        for copy, k in gb_stage(stage):
            copy.wait_recv()
            total = total + gbs[4 + k]
        gbs[stage + 1] = total

    def gathered(c):
        if not fused:
            for copy in w_copies(c):
                copy.wait()
            return
        for y in range(1, plane):
            a2(c, y).wait_recv()
        a3(c).start()
        if c + 1 < n_chunks:
            for x in range(1, span):
                a1(c + 1, x).wait_recv()
            for y in range(1, plane):
                a2(c + 1, y).start()
        a3(c).wait_recv()

    for c in range(n_chunks):
        gathered(c)
        pass_a(c)
    if fused:
        gbs[0] = jnp.zeros(gbs.shape[1:], F32)
    for c in range(n_chunks):
        pass_b(c)
        if fused and c:
            r2(c - 1, 1)
        if fused and c == n_chunks - 1:
            gb_go(0)
        pass_c(c, 0)
        if fused and c:
            r3(c - 1, 0)
        pass_c(c, 1)
        if fused:
            if c:
                r3(c - 1, 1)
            r2(c, 0)
            if c > 1:
                r4(c - 2)
    out_h = pltpu.make_async_copy(raw_t, hid, out_sem.at[0])
    out_h.start()

    to_left = remote(edge.at[2], edge.at[3], edge_send.at[1], edge_recv.at[1], (me - 1, col))

    @pl.when(me == span - 1)
    def _():
        edge[3] = jnp.zeros((seqs, width), F32)

    def put(b):
        at = mult(b * block, block)
        out = dot(pinv[...], gates[pl.ds(at, block), :width].astype(BF)).astype(BF)
        raw_u[:, pl.ds(mult(b * STEPS, STEPS), STEPS), :] = out.reshape(seqs, STEPS, width)

    def late_links(i):
        last = n_chunks - 1
        plan = {
            1: [lambda: r2(last, 1), lambda: r5(max(0, last - 2)), lambda: gb_sum(0), lambda: gb_go(1)],
            3: [lambda: r3(last, 0), lambda: r4(last - 1), lambda: gb_sum(1), lambda: gb_go(2)],
            5: [lambda: r3(last, 1), lambda: r5(last - 1), lambda: gb_sum(2)],
        }
        for when, todo in plan.items():

            @pl.when(i == when)
            def _(todo=todo):
                for step in todo:
                    step()

    def inputs(i, pend):
        r0 = mult(i * block, block)
        both = dot_columns(gp[pl.ds(r0, block), :], weights_of(0, 3 * width))
        own = both[:, :width]
        late = both[:, width:] * wide_keep(r0, block, width)
        gates[pl.ds(r0, block - seqs), :width] = own[: block - seqs] + late[seqs:]

        @pl.when(i == 0)
        def _():
            edge[2] = late[:seqs]

            @pl.when(me > 0)
            def _():
                to_left.start()

        @pl.when(i > 0)
        def _():
            gates[pl.ds(mult(r0 - seqs, seqs), seqs), :width] = pend + late[:seqs]
            put(i - 1)

        if fused:
            late_links(i)
        return own[block - seqs :]

    pend = lax.fori_loop(0, blocks, inputs, jnp.zeros((seqs, width), F32))

    @pl.when(me < span - 1)
    def _():
        to_left.wait_recv()

    @pl.when(me > 0)
    def _():
        to_left.wait_send()

    gates[rows - seqs :, :width] = pend + edge[3]
    put(blocks - 1)
    out_t = pltpu.make_async_copy(raw_u, gtok, out_sem.at[1])
    out_t.start()
    if not fused:
        for turn in (0, 1):
            for copy in gw_copies(n_chunks - 1, turn):
                copy.wait()
    else:
        last = n_chunks - 1
        r4(last)
        for g in range(3 * width // LANES):
            gb[0:1, g * LANES : (g + 1) * LANES] = gbs[3, g : g + 1, :]
        r5(last)
        a0.wait_send()
        for c in range(n_chunks):
            a3(c).wait_send()
            for x in range(1, span):
                a1(c, x).wait_send()
            for y in range(1, plane):
                a2(c, y).wait_send()
            for turn in (0, 1):
                for n, x in enumerate(orders(turn)):
                    for y in range(1, plane):
                        r2_copy(c, turn, n, y).wait_send()
                    if x:
                        r3_copy(c, turn, n).wait_send()
            if chunks[c][1] != LANES:
                r4_copy(c).wait_send()
        for turn in (0, 1):
            r1_copy(last, turn).wait_send()
        for stage_index in range(3):
            for copy, _ in gb_stage(stage_index):
                copy.wait_send()
    out_h.wait()
    out_t.wait()


def per_device(tokens, weights, bias, resets, upstream):
    seqs, steps, width = tokens.shape
    rows = seqs * steps
    span, peers = lax.axis_size("seq"), lax.axis_size("dp")
    chunks = cut_chunks(width)
    n_chunks = len(chunks)
    block = seqs * STEPS
    depth = 2 * width
    shard = weights.shape[0]
    slab = 2 * shard
    plane = peers // 2
    half = span // 2
    fused = shard % 8 == 0 and slab % 16 == 0 and n_chunks >= 3 and steps // STEPS >= 6
    any_spec = pl.BlockSpec(memory_space=pl.ANY)
    vmem = pl.BlockSpec(memory_space=pltpu.VMEM)
    dma = pltpu.SemaphoreType.DMA
    if fused:
        w_shape, c_shape, w_sems = (span, plane, slab, 3 * width), (2, half * plane, slab, 2 * TRIO), (1,)
        gw_shape, gw_spec = (shard, 3 * width), vmem
        links = [
            pltpu.VMEM((shard, 3 * width), BF),
            pltpu.VMEM((2, shard, 3 * width), F32),
            pltpu.VMEM((2, half * plane, slab, TRIO), BF),
            pltpu.VMEM((n_chunks, 2, half * plane, slab, TRIO), BF),
            pltpu.VMEM((n_chunks, 2, half, plane - 1, slab, TRIO), BF),
            pltpu.VMEM((n_chunks, 2, half, slab, TRIO), F32),
            pltpu.VMEM((n_chunks, span - 1, slab, TRIO), BF),
            pltpu.VMEM((n_chunks, slab, TRIO), F32),
            pltpu.VMEM((n_chunks, shard, TRIO), F32),
            pltpu.VMEM((4 + span + plane - 1, 16, LANES), F32),
            dma((2,)),
            dma((n_chunks, span - 1)),
            dma((n_chunks, span - 1)),
            dma((n_chunks, plane - 1)),
            dma((n_chunks, plane - 1)),
            dma((n_chunks, 2)),
            dma((n_chunks, 2)),
            dma((n_chunks, 2)),
            dma((n_chunks, 2, half, plane - 1)),
            dma((n_chunks, 2, half, plane - 1)),
            dma((n_chunks, span - 1)),
            dma((n_chunks, span - 1)),
            dma((n_chunks, 2)),
            dma((span + plane - 1,)),
            dma((span + plane - 1,)),
        ]
    else:
        weights = lax.all_gather(weights, ("seq", "dp"), axis=0, tiled=True)
        w_shape, c_shape, w_sems = (depth, 3 * width), (2, depth // 2, 2 * TRIO), (n_chunks, 3, 2)
        gw_shape, gw_spec = (depth, 3 * width), any_spec
        links = []
    hid, gtok, gw, gb = pl.pallas_call(
        functools.partial(layer_kernel, span, peers, fused, chunks),
        out_shape=(
            jax.ShapeDtypeStruct(tokens.shape, BF),
            jax.ShapeDtypeStruct(tokens.shape, BF),
            jax.ShapeDtypeStruct(gw_shape, F32),
            jax.ShapeDtypeStruct((1, 3 * width), F32),
        ),
        in_specs=[any_spec, any_spec, vmem, vmem, any_spec],
        out_specs=(any_spec, any_spec, gw_spec, vmem),
        scratch_shapes=[
            pltpu.VMEM(tokens.shape, BF),
            pltpu.VMEM(tokens.shape, BF),
            pltpu.VMEM((rows, depth), BF),
            pltpu.VMEM((rows, width), BF),
            pltpu.VMEM(w_shape, BF),
            pltpu.VMEM((rows, 3 * width), F32),
            pltpu.VMEM((rows, 2 * LANES), F32),
            pltpu.VMEM((rows, 3 * width), BF),
            pltpu.VMEM((rows, LANES), F32),
            pltpu.VMEM((block, block), BF),
            pltpu.VMEM((block, block), BF),
            pltpu.VMEM((block, 2 * LANES), BF),
            pltpu.VMEM(c_shape, F32),
            pltpu.VMEM((span, 3 * seqs, width), F32),
            pltpu.VMEM((4, seqs, width), F32),
            dma((2,)),
            dma(w_sems),
            dma((2,)),
            dma((n_chunks, span - 1)),
            dma((n_chunks, span - 1)),
            dma((2,)),
            dma((2,)),
        ]
        + links,
        compiler_params=pltpu.CompilerParams(
            collective_id=0, has_side_effects=True, vmem_limit_bytes=62 << 20
        ),
        name="layer",
    )(tokens, weights, bias.reshape(1, -1), resets, upstream)
    if not fused:
        gw = lax.psum_scatter(gw, ("seq", "dp"), scatter_dimension=0, tiled=True)
        gb = lax.psum(gb, ("seq", "dp"))
    return hid, gtok, gw, gb[0]


def solution(mesh):
    spread = P("dp", "seq", None)
    rows = P(("seq", "dp"), None)
    return jax.shard_map(
        per_device,
        mesh=mesh,
        in_specs=(spread, rows, P(), P("dp", "seq"), spread),
        out_specs=(spread, spread, rows, P()),
        check_vma=False,
    )
```

time: 299 us -> 119 us (0.40)
  waiting for transfers between devices: 167 us -> 0 us
  blocking collectives: 38.4 us -> 0 us
  Pallas kernels: 72.2 us -> 110 us
  between operations: 14.1 us -> 0.64 us
    unnamed x3 -> x0, waiting for transfers between devices: 98.4 us -> none
    all_gather x1 -> x0, waiting for transfers between devices: 68.8 us -> none  [per_device(): full = lax.all_gather(weights, ('seq', 'dp'), axis=0, tiled=True)]
    psum x1 -> x0, blocking collectives: 38.4 us -> none  [per_device(): gb = lax.psum(gb[0], ('seq', 'dp'))]
    pallas_call x1, Pallas kernels: 72.2 us -> 110 us  [per_device(): pl.pallas_call(functools.partial(layer_kernel, span, peers, fused, chunks...]
  transfers between devices with their start and end apart: 2 -> 0, of which waited for: 2 -> 0; matrix products, arithmetic and copies ran while one was open for 0% -> 0% of each run, Pallas kernels for 0% -> 0%
where the time goes in v2:
time: 119 us
  Pallas kernels  110 us (92%)
  local copies, waits for them, and re-layouts  7.17 us (6%)
  other arithmetic  1.32 us (1%)
    pallas_call x1, Pallas kernels, per_device(): pl.pallas_call(functools.partial(layer_kernel, span, peers, fused, chunks...  110 us
    unnamed x7, local copies, waits for them, and re-layouts  5.87 us

profile of v2, /device:TPU:0, one launch (start us, length us, event | category | flops | bytes accessed | tf_op | source)
XLA Modules:
  0.0 119.0 jit_solution(10560710034339554615)
XLA Ops:
  0.6 1.3 %reshape.11.bias = f32[1,1920]{1,0:T(1,128)} reshape(f32[1920]{0:T(1024)} %param.7) | data formatting | bytes 15360 | tf_op jit(solution)/shard_map/reshape | solution.py:761
  1.9 109.9 %layer.1 = (bf16[8,256,640]{2,1,0:T(8,128)(2,1)}, bf16[8,256,640]{2,1,0:T(8,128)(2,1)}, f32[40,1920]{1,0:T(8,128)}, f32[1,1920]{1,0:T(1,128)}) custom-call(bf16[8,256,640]{2,1,0:T(8,128)(2,1)} %tok.1, bf16[40,1920]{1,0:T(8,128)(2,1)} %wts.1, f32[1,1920]{1,0:T(1,128)} %reshape.11.bias, s32[8,256]{1,0:T(8,128)} %resets.1, bf16[8,256,640]{2,1,0:T(8,128)(2,1)} %up.1), custom_call_target="tpu_custom_call" | custom-call | tf_op jit(solution)/shard_map/layer/pallas_call | solution.py:722
  111.8 1.3 %reduce = f32[1920]{0:T(1024)} reduce(f32[1,1920]{1,0:T(1,128)} %get-tuple-element.11, f32[]{:T(128)} %constant.1), dimensions={0}, to_apply=%get-tuple-element.11.reduce_sub_computation | reduce | bytes 15364 | tf_op jit(solution)/shard_map/layer/pallas_call | solution.py:722
  113.1 0.0 copy-start
  113.1 3.7 %copy.12 = bf16[8,256,640]{2,1,0:T(8,128)(2,1)} copy(bf16[8,256,640]{2,1,0:T(8,128)(2,1)} %get-tuple-element.16) | data formatting | bytes 5242880
  116.8 0.0 copy-done
  116.8 0.0 copy-start.1
  116.8 1.5 %copy.13 = bf16[8,256,640]{2,1,0:T(8,128)(2,1)} copy(bf16[8,256,640]{2,1,0:T(8,128)(2,1)S(1)} %copy-done) | data formatting | bytes 5242880
  118.3 0.0 copy-done.1
  118.3 0.7 copy.14
Async XLA Ops:
  113.1 3.7 %copy-start = (bf16[8,256,640]{2,1,0:T(8,128)(2,1)S(1)}, bf16[8,256,640]{2,1,0:T(8,128)(2,1)}, u32[]{:S(2)}) copy-start(bf16[8,256,640]{2,1,0:T(8,128)(2,1)} %get-tuple-element.17) | copy-start | bytes 7864324
  116.8 1.5 %copy-start.1 = (f32[40,1920]{1,0:T(8,128)S(1)}, f32[40,1920]{1,0:T(8,128)}, u32[]{:S(2)}) copy-start(f32[40,1920]{1,0:T(8,128)} %get-tuple-element.18) | copy-start | bytes 921604

commit v3 on v2

--- a/solution.py
+++ b/solution.py
@@ -1,4 +1,5 @@
 import functools
+import types
 
 import jax
 import jax.numpy as jnp
@@ -14,6 +15,7 @@
 TRIO = 3 * LANES
 STEPS = 32
 TWO = 16
+VMEM_BYTES = 56 << 20
 
 
 def cut_chunks(width):
@@ -41,13 +43,19 @@
 
 
 def layer_kernel(
-    span, peers, fused, chunks,
+    span, peers, fused, chunks, names,
     tok, wts, bias, resets, up,
     hid, gtok, gw, gb,
-    raw_t, raw_u, joined, upt, wv, gates, qf, gp, keepb, perm, pinv, hb, cbuf, summ, edge,
-    in_sem, w_sem, out_sem, sum_send, sum_recv, edge_send, edge_recv,
-    *links,
+    *scratch,
 ):
+    held = types.SimpleNamespace(**dict(zip(names, scratch)))
+    joined, upt, wv, qf, keepb = held.joined, held.upt, held.wv, held.qf, held.keepb
+    perm, pinv, cbuf, summ, edge = held.perm, held.pinv, held.cbuf, held.summ, held.edge
+    in_sem, w_sem = held.in_sem, held.w_sem
+    sum_send, sum_recv = held.sum_send, held.sum_recv
+    edge_send, edge_recv = held.edge_send, held.edge_recv
+    gates = [getattr(held, f"gates{c}") for c in range(len(chunks))]
+    gp = [getattr(held, f"gp{c}") for c in range(len(chunks))]
     seqs, steps, width = tok.shape
     rows = seqs * steps
     block = seqs * STEPS
@@ -65,11 +73,12 @@
     over = -(-shard // 16) * 16
     partner = (me, col ^ 1)
     if fused:
-        (
-            own16, pair, sb1, rb1, rb2, own2, rb3, fin, fin_rx, gbs,
-            a0_sem, a1_send, a1_recv, a2_send, a2_recv, a3_sem,
-            r1_send, r1_recv, r2_send, r2_recv, r3_send, r3_recv, r4_sem, gb_send, gb_recv,
-        ) = links
+        own16, pair, sb1, rb1, rb2 = held.own16, held.pair, held.sb1, held.rb1, held.rb2
+        own2, rb3, fin, fin_rx, gbs = held.own2, held.rb3, held.fin, held.fin_rx, held.gbs
+        a0_sem, a3_sem, r4_sem = held.a0_sem, held.a3_sem, held.r4_sem
+        a1_send, a1_recv, a2_send, a2_recv = held.a1_send, held.a1_recv, held.a2_send, held.a2_recv
+        r1_send, r1_recv, r2_send, r2_recv = held.r1_send, held.r1_recv, held.r2_send, held.r2_recv
+        r3_send, r3_recv, gb_send, gb_recv = held.r3_send, held.r3_recv, held.gb_send, held.gb_recv
 
     def remote(src, dst, send, recv, to):
         return pltpu.make_async_remote_copy(
@@ -80,8 +89,8 @@
     def mult(v, m):
         return pl.multiple_of(v, m)
 
-    in_t = pltpu.make_async_copy(tok, raw_t, in_sem.at[0])
-    in_u = pltpu.make_async_copy(up, raw_u, in_sem.at[1])
+    in_t = pltpu.make_async_copy(tok, hid, in_sem.at[0])
+    in_u = pltpu.make_async_copy(up, gtok, in_sem.at[1])
     if fused:
         in_w = pltpu.make_async_copy(wts, own16, w_sem.at[0])
         in_w.start()
@@ -179,7 +188,7 @@
         return jnp.concatenate([k] * (lanes // LANES), axis=1)
 
     in_t.wait()
-    last_rows = raw_t[:, steps - STEPS :, :].reshape(block, width)
+    last_rows = hid[:, steps - STEPS :, :].reshape(block, width)
     edge[0] = dot(perm[block - TWO :, :], last_rows)[TWO - seqs :]
     to_right = remote(edge.at[0], edge.at[1], edge_send.at[0], edge_recv.at[0], (me + 1, col))
 
@@ -200,13 +209,13 @@
 
     def stage(b, last):
         at = mult(b * block, block)
-        src = raw_t[:, pl.ds(mult(b * STEPS, STEPS), STEPS), :].reshape(block, width)
+        src = hid[:, pl.ds(mult(b * STEPS, STEPS), STEPS), :].reshape(block, width)
         now = dot(perm[...], src)
         before = jnp.concatenate([last, now[: block - seqs]], axis=0)
         before = before * wide_keep(at, block, width)
         joined[pl.ds(at, block), :width] = now.astype(BF)
         joined[pl.ds(at, block), width:] = before.astype(BF)
-        src = raw_u[:, pl.ds(mult(b * STEPS, STEPS), STEPS), :].reshape(block, width)
+        src = gtok[:, pl.ds(mult(b * STEPS, STEPS), STEPS), :].reshape(block, width)
         upt[pl.ds(at, block), :] = dot(perm[...], src).astype(BF)
         return now[block - seqs :]
 
@@ -236,7 +245,7 @@
 
         def bias_rows(g, h):
             lane = g * width + at + h * LANES
-            return jnp.broadcast_to(bias[0:1, lane : lane + LANES], (TWO, LANES))
+            return jnp.broadcast_to(bias[lane : lane + LANES].reshape(1, LANES), (TWO, LANES))
 
         bias_z = [bias_rows(0, h) for h in halves]
         bias_f = [0.5 * bias_rows(1, h) for h in halves]
@@ -245,20 +254,19 @@
         def body(i, carry):
             carry = [list(v) for v in carry]
             r0 = mult(i * size, size)
-            gates[pl.ds(r0, size), base : base + 3 * cw] = dot(
-                joined[pl.ds(r0, size), :], weights_of(base, 3 * cw)
-            )
+            pre = dot(joined[pl.ds(r0, size), :], weights_of(base, 3 * cw))
             for j in range(size // TWO):
                 sl = pl.ds(r0 + j * TWO, TWO)
                 k = keepb[sl, :]
                 for h in halves:
-                    zc, fc, oc = (base + h * TRIO + g * LANES for g in range(3))
-                    z = jnp.tanh(gates[sl, zc : zc + LANES] + bias_z[h])
-                    f = 0.5 * jnp.tanh(0.5 * gates[sl, fc : fc + LANES] + bias_f[h]) + 0.5
-                    o = 0.5 * jnp.tanh(0.5 * gates[sl, oc : oc + LANES] + bias_o[h]) + 0.5
-                    gates[sl, zc : zc + LANES] = z
-                    gates[sl, fc : fc + LANES] = f
-                    gates[sl, oc : oc + LANES] = o
+                    zc, fc, oc = (h * TRIO + g * LANES for g in range(3))
+                    now = pre[j * TWO : (j + 1) * TWO]
+                    z = jnp.tanh(now[:, zc : zc + LANES] + bias_z[h])
+                    f = 0.5 * jnp.tanh(0.5 * now[:, fc : fc + LANES] + bias_f[h]) + 0.5
+                    o = 0.5 * jnp.tanh(0.5 * now[:, oc : oc + LANES] + bias_o[h]) + 0.5
+                    gates[c][sl, zc : zc + LANES] = z
+                    gates[c][sl, fc : fc + LANES] = f
+                    gates[c][sl, oc : oc + LANES] = o
                     g = upt[sl, at + h * LANES : at + (h + 1) * LANES].astype(F32)
                     eff = f * k
                     fresh = (1.0 - f) * z
@@ -290,7 +298,6 @@
 
     def pass_b(c):
         at, cw = chunks[c]
-        base = 3 * at
         halves = range(cw // LANES)
         for k in range(1, span):
             exchange(c, k).wait()
@@ -315,11 +322,12 @@
                 sl = pl.ds(r0 + j * TWO, TWO)
                 k = keepb[sl, :]
                 for h in halves:
-                    zc, fc, oc = (base + h * TRIO + g * LANES for g in range(3))
-                    z = gates[sl, zc : zc + LANES]
-                    f = gates[sl, fc : fc + LANES]
-                    o = gates[sl, oc : oc + LANES]
-                    g = upt[sl, at + h * LANES : at + (h + 1) * LANES].astype(F32)
+                    zc, fc, oc = (h * TRIO + g * LANES for g in range(3))
+                    z = gates[c][sl, zc : zc + LANES]
+                    f = gates[c][sl, fc : fc + LANES]
+                    o = gates[c][sl, oc : oc + LANES]
+                    lanes = slice(at + h * LANES, at + (h + 1) * LANES)
+                    g = upt[sl, lanes].astype(F32)
                     eff = f * k
                     rest = 1.0 - f
                     fresh = rest * z
@@ -328,17 +336,17 @@
                     cell = jnp.concatenate([c0, c1], axis=0)
                     prev = jnp.concatenate([cells[h], c0], axis=0)
                     cells[h] = c1
-                    hb[j * TWO : (j + 1) * TWO, h * LANES : (h + 1) * LANES] = (o * cell).astype(BF)
+                    hid[j // 2, pl.ds(mult(i * STEPS + j % 2 * TWO, TWO), TWO), lanes] = (
+                        o * cell
+                    ).astype(BF)
                     src = g * o
                     go = src * cell * (1.0 - o)
-                    gp[sl, oc : oc + LANES] = go.astype(BF)
+                    gp[c][sl, oc : oc + LANES] = go.astype(BF)
                     sums[h] = sums[h] + go
-                    gates[sl, zc : zc + LANES] = rest * (1.0 - z * z)
-                    gates[sl, fc : fc + LANES] = eff
-                    gates[sl, oc : oc + LANES] = src
+                    gates[c][sl, zc : zc + LANES] = rest * (1.0 - z * z)
+                    gates[c][sl, fc : fc + LANES] = eff
+                    gates[c][sl, oc : oc + LANES] = src
                     qf[sl, h * LANES : (h + 1) * LANES] = (prev * k - z) * (f * rest)
-            out = dot(pinv[...], hb[:, :cw]).astype(BF).reshape(seqs, STEPS, cw)
-            raw_t[:, pl.ds(mult(i * STEPS, STEPS), STEPS), at : at + cw] = out
             return tuple(cells), tuple(sums)
 
         zero = jnp.zeros((TWO, LANES), F32)
@@ -351,17 +359,17 @@
             for j in range(block // TWO - 1, -1, -1):
                 sl = pl.ds(r0 + j * TWO, TWO)
                 for h in halves:
-                    zc, fc, oc = (base + h * TRIO + g * LANES for g in range(3))
-                    eff = gates[sl, fc : fc + LANES]
-                    src = gates[sl, oc : oc + LANES]
+                    zc, fc, oc = (h * TRIO + g * LANES for g in range(3))
+                    eff = gates[c][sl, fc : fc + LANES]
+                    src = gates[c][sl, oc : oc + LANES]
                     g1 = src[seqs:] + heads[h]
                     g0 = src[:seqs] + eff[seqs:] * g1
                     heads[h] = eff[:seqs] * g0
                     gc = jnp.concatenate([g0, g1], axis=0)
-                    gz = gc * gates[sl, zc : zc + LANES]
+                    gz = gc * gates[c][sl, zc : zc + LANES]
                     gf = gc * qf[sl, h * LANES : (h + 1) * LANES]
-                    gp[sl, zc : zc + LANES] = gz.astype(BF)
-                    gp[sl, fc : fc + LANES] = gf.astype(BF)
+                    gp[c][sl, zc : zc + LANES] = gz.astype(BF)
+                    gp[c][sl, fc : fc + LANES] = gf.astype(BF)
                     sums_z[h] = sums_z[h] + gz
                     sums_f[h] = sums_f[h] + gf
             return tuple(heads), tuple(sums_z), tuple(sums_f)
@@ -375,7 +383,7 @@
                     gbs[0, tile : tile + 1, :] = line
                 else:
                     lane = g * width + at + h * LANES
-                    gb[0:1, lane : lane + LANES] = line
+                    gb[lane : lane + LANES] = line.reshape(LANES)
 
     def gw_copies(c, turn):
         at, cw = chunks[c]
@@ -391,26 +399,29 @@
 
     def pass_c(c, turn):
         at, cw = chunks[c]
-        base = 3 * at
         if fused:
             r0 = mult(((me // (span // 2)) ^ 1 ^ turn) * half_rows, LANES)
-            result = dot_rows(joined[:, pl.ds(r0, half_rows)], gp[:, base : base + 3 * cw])
-            cbuf[turn, :, :, : 3 * cw] = result.reshape(-1, slab, 3 * cw)
-            r1(c, turn)
+            if c:
+                r1_copy(c - 1, turn).wait_send()
+            result = dot_rows(joined[:, pl.ds(r0, half_rows)], gp[c][...])
+            result = result.reshape(-1, slab, 3 * cw)
+            count = carried(c, 0)[0]
+            if cw == LANES:
+                zero, one = result[:, :count], result[:, slab - count :]
+            else:
+                zero, one = result[:, :, :TRIO], result[:, :, TRIO:]
+            cbuf[turn, :, :count] = jnp.where(core == 0, zero, one)
+            sb1[turn, :, :count] = jnp.where(core == 0, one, zero).astype(BF)
+            r1_copy(c, turn).start()
         else:
             if c:
                 for copy in gw_copies(c - 1, turn):
                     copy.wait()
             cbuf[turn, :, : 3 * cw] = dot_rows(
-                joined[:, turn * half_rows : (turn + 1) * half_rows], gp[:, base : base + 3 * cw]
+                joined[:, turn * half_rows : (turn + 1) * half_rows], gp[c][...]
             )
             for copy in gw_copies(c, turn):
                 copy.start()
-
-    def own_part(c, who):
-        count, r0, _ = carried(c, who)
-        c0 = 0 if chunks[c][1] == LANES else mult(TRIO * who, LANES)
-        return pl.ds(r0, count), pl.ds(c0, TRIO)
 
     def part_rows(c):
         return pl.ds(0, carried(c, 0)[0])
@@ -425,13 +436,6 @@
             sb1.at[turn, :, k], rb1.at[c, turn, :, k], r1_send.at[c, turn], r1_recv.at[c, turn],
             partner,
         )
-
-    def r1(c, turn):
-        if c:
-            r1_copy(c - 1, turn).wait_send()
-        rs, cs = own_part(c, 1 - core)
-        sb1[turn, :, part_rows(c), :] = cbuf[turn, :, rs, cs].astype(BF)
-        r1_copy(c, turn).start()
 
     def r2_copy(c, turn, n, y):
         k = part_rows(c)
@@ -445,11 +449,10 @@
     def r2(c, turn):
         r1_copy(c, turn).wait_recv()
         k = part_rows(c)
-        rs, cs = own_part(c, core)
         for n, x in enumerate(orders(turn)):
             for y in range(plane - 1, -1, -1):
                 index = ((me ^ x) % (span // 2)) * plane + (place ^ y)
-                total = cbuf[turn, index, rs, cs] + rb1[c, turn, index, k].astype(F32)
+                total = cbuf[turn, index, k] + rb1[c, turn, index, k].astype(F32)
                 if y:
                     rb1[c, turn, index, k] = total.astype(BF)
                     r2_copy(c, turn, n, y).start()
@@ -547,16 +550,20 @@
                 a2(c + 1, y).start()
         a3(c).wait_recv()
 
-    for c in range(n_chunks):
+    def gates_of(c):
         gathered(c)
         pass_a(c)
+
+    last = n_chunks - 1
     if fused:
         gbs[0] = jnp.zeros(gbs.shape[1:], F32)
+    gates_of(0)
+    gates_of(1)
     for c in range(n_chunks):
         pass_b(c)
         if fused and c:
             r2(c - 1, 1)
-        if fused and c == n_chunks - 1:
+        if fused and c == last:
             gb_go(0)
         pass_c(c, 0)
         if fused and c:
@@ -568,8 +575,8 @@
             r2(c, 0)
             if c > 1:
                 r4(c - 2)
-    out_h = pltpu.make_async_copy(raw_t, hid, out_sem.at[0])
-    out_h.start()
+        if c + 2 < n_chunks:
+            gates_of(c + 2)
 
     to_left = remote(edge.at[2], edge.at[3], edge_send.at[1], edge_recv.at[1], (me - 1, col))
 
@@ -577,13 +584,19 @@
     def _():
         edge[3] = jnp.zeros((seqs, width), F32)
 
+    late_gt = gates[last]
+
+    def settle(ref, b, value):
+        out = dot(pinv[...], value).astype(BF)
+        ref[:, pl.ds(mult(b * STEPS, STEPS), STEPS), :] = out.reshape(seqs, STEPS, width)
+
     def put(b):
-        at = mult(b * block, block)
-        out = dot(pinv[...], gates[pl.ds(at, block), :width].astype(BF)).astype(BF)
-        raw_u[:, pl.ds(mult(b * STEPS, STEPS), STEPS), :] = out.reshape(seqs, STEPS, width)
+        settle(gtok, b, late_gt[pl.ds(mult(b * block, block), block), :width].astype(BF))
+
+    def put_hidden(b):
+        settle(hid, b, hid[:, pl.ds(mult(b * STEPS, STEPS), STEPS), :].reshape(block, width))
 
     def late_links(i):
-        last = n_chunks - 1
         plan = {
             1: [lambda: r2(last, 1), lambda: r5(max(0, last - 2)), lambda: gb_sum(0), lambda: gb_go(1)],
             3: [lambda: r3(last, 0), lambda: r4(last - 1), lambda: gb_sum(1), lambda: gb_go(2)],
@@ -598,10 +611,15 @@
 
     def inputs(i, pend):
         r0 = mult(i * block, block)
-        both = dot_columns(gp[pl.ds(r0, block), :], weights_of(0, 3 * width))
+        put_hidden(i)
+        put(jnp.maximum(i - 2, 0))
+        grads = jnp.concatenate([g[pl.ds(r0, block), :] for g in gp], axis=1)
+        both = dot_columns(grads, weights_of(0, 3 * width))
         own = both[:, :width]
         late = both[:, width:] * wide_keep(r0, block, width)
-        gates[pl.ds(r0, block - seqs), :width] = own[: block - seqs] + late[seqs:]
+        late_gt[pl.ds(r0, block - seqs), :width] = own[: block - seqs] + late[seqs:]
+        before = jnp.where(i == 0, rows - seqs, r0 - seqs)
+        late_gt[pl.ds(mult(before, seqs), seqs), :width] = pend + late[:seqs]
 
         @pl.when(i == 0)
         def _():
@@ -611,11 +629,6 @@
             def _():
                 to_left.start()
 
-        @pl.when(i > 0)
-        def _():
-            gates[pl.ds(mult(r0 - seqs, seqs), seqs), :width] = pend + late[:seqs]
-            put(i - 1)
-
         if fused:
             late_links(i)
         return own[block - seqs :]
@@ -630,19 +643,17 @@
     def _():
         to_left.wait_send()
 
-    gates[rows - seqs :, :width] = pend + edge[3]
+    late_gt[rows - seqs :, :width] = pend + edge[3]
+    put(blocks - 2)
     put(blocks - 1)
-    out_t = pltpu.make_async_copy(raw_u, gtok, out_sem.at[1])
-    out_t.start()
     if not fused:
         for turn in (0, 1):
             for copy in gw_copies(n_chunks - 1, turn):
                 copy.wait()
     else:
-        last = n_chunks - 1
         r4(last)
         for g in range(3 * width // LANES):
-            gb[0:1, g * LANES : (g + 1) * LANES] = gbs[3, g : g + 1, :]
+            gb[g * LANES : (g + 1) * LANES] = gbs[3, g : g + 1, :].reshape(LANES)
         r5(last)
         a0.wait_send()
         for c in range(n_chunks):
@@ -664,8 +675,6 @@
         for stage_index in range(3):
             for copy, _ in gb_stage(stage_index):
                 copy.wait_send()
-    out_h.wait()
-    out_t.wait()
 
 
 def per_device(tokens, weights, bias, resets, upstream):
@@ -684,85 +693,86 @@
     any_spec = pl.BlockSpec(memory_space=pl.ANY)
     vmem = pl.BlockSpec(memory_space=pltpu.VMEM)
     dma = pltpu.SemaphoreType.DMA
+    vm = pltpu.VMEM
+    held = {
+        "joined": vm((rows, depth), BF),
+        "upt": vm((rows, width), BF),
+        "qf": vm((rows, 2 * LANES), F32),
+        "keepb": vm((rows, LANES), F32),
+        "perm": vm((block, block), BF),
+        "pinv": vm((block, block), BF),
+        "summ": vm((span, 3 * seqs, width), F32),
+        "edge": vm((4, seqs, width), F32),
+        "in_sem": dma((2,)),
+        "sum_send": dma((n_chunks, span - 1)),
+        "sum_recv": dma((n_chunks, span - 1)),
+        "edge_send": dma((2,)),
+        "edge_recv": dma((2,)),
+    }
+    for c, (_, cw) in enumerate(chunks):
+        held[f"gates{c}"] = vm((rows, 3 * cw), F32)
+        held[f"gp{c}"] = vm((rows, 3 * cw), BF)
     if fused:
-        w_shape, c_shape, w_sems = (span, plane, slab, 3 * width), (2, half * plane, slab, 2 * TRIO), (1,)
         gw_shape, gw_spec = (shard, 3 * width), vmem
-        links = [
-            pltpu.VMEM((shard, 3 * width), BF),
-            pltpu.VMEM((2, shard, 3 * width), F32),
-            pltpu.VMEM((2, half * plane, slab, TRIO), BF),
-            pltpu.VMEM((n_chunks, 2, half * plane, slab, TRIO), BF),
-            pltpu.VMEM((n_chunks, 2, half, plane - 1, slab, TRIO), BF),
-            pltpu.VMEM((n_chunks, 2, half, slab, TRIO), F32),
-            pltpu.VMEM((n_chunks, span - 1, slab, TRIO), BF),
-            pltpu.VMEM((n_chunks, slab, TRIO), F32),
-            pltpu.VMEM((n_chunks, shard, TRIO), F32),
-            pltpu.VMEM((4 + span + plane - 1, 16, LANES), F32),
-            dma((2,)),
-            dma((n_chunks, span - 1)),
-            dma((n_chunks, span - 1)),
-            dma((n_chunks, plane - 1)),
-            dma((n_chunks, plane - 1)),
-            dma((n_chunks, 2)),
-            dma((n_chunks, 2)),
-            dma((n_chunks, 2)),
-            dma((n_chunks, 2, half, plane - 1)),
-            dma((n_chunks, 2, half, plane - 1)),
-            dma((n_chunks, span - 1)),
-            dma((n_chunks, span - 1)),
-            dma((n_chunks, 2)),
-            dma((span + plane - 1,)),
-            dma((span + plane - 1,)),
-        ]
+        piece = (half * plane, slab, TRIO)
+        held |= {
+            "wv": vm((span, plane, slab, 3 * width), BF),
+            "cbuf": vm((2, *piece), F32),
+            "own16": vm((shard, 3 * width), BF),
+            "pair": vm((2, shard, 3 * width), F32),
+            "sb1": vm((2, *piece), BF),
+            "rb1": vm((n_chunks, 2, *piece), BF),
+            "rb2": vm((n_chunks, 2, half, plane - 1, slab, TRIO), BF),
+            "own2": vm((n_chunks, 2, half, slab, TRIO), F32),
+            "rb3": vm((n_chunks, span - 1, slab, TRIO), BF),
+            "fin": vm((n_chunks, slab, TRIO), F32),
+            "fin_rx": vm((n_chunks, shard, TRIO), F32),
+            "gbs": vm((4 + span + plane - 1, 16, LANES), F32),
+            "w_sem": dma((1,)),
+            "a0_sem": dma((2,)),
+            "a1_send": dma((n_chunks, span - 1)),
+            "a1_recv": dma((n_chunks, span - 1)),
+            "a2_send": dma((n_chunks, plane - 1)),
+            "a2_recv": dma((n_chunks, plane - 1)),
+            "a3_sem": dma((n_chunks, 2)),
+            "r1_send": dma((n_chunks, 2)),
+            "r1_recv": dma((n_chunks, 2)),
+            "r2_send": dma((n_chunks, 2, half, plane - 1)),
+            "r2_recv": dma((n_chunks, 2, half, plane - 1)),
+            "r3_send": dma((n_chunks, span - 1)),
+            "r3_recv": dma((n_chunks, span - 1)),
+            "r4_sem": dma((n_chunks, 2)),
+            "gb_send": dma((span + plane - 1,)),
+            "gb_recv": dma((span + plane - 1,)),
+        }
     else:
         weights = lax.all_gather(weights, ("seq", "dp"), axis=0, tiled=True)
-        w_shape, c_shape, w_sems = (depth, 3 * width), (2, depth // 2, 2 * TRIO), (n_chunks, 3, 2)
         gw_shape, gw_spec = (depth, 3 * width), any_spec
-        links = []
+        held |= {
+            "wv": vm((depth, 3 * width), BF),
+            "cbuf": vm((2, depth // 2, 2 * TRIO), F32),
+            "w_sem": dma((n_chunks, 3, 2)),
+        }
     hid, gtok, gw, gb = pl.pallas_call(
-        functools.partial(layer_kernel, span, peers, fused, chunks),
+        functools.partial(layer_kernel, span, peers, fused, chunks, tuple(held)),
         out_shape=(
-            jax.ShapeDtypeStruct(tokens.shape, BF),
-            jax.ShapeDtypeStruct(tokens.shape, BF),
+            vm(tokens.shape, BF),
+            vm(tokens.shape, BF),
             jax.ShapeDtypeStruct(gw_shape, F32),
-            jax.ShapeDtypeStruct((1, 3 * width), F32),
+            jax.ShapeDtypeStruct((3 * width,), F32),
         ),
         in_specs=[any_spec, any_spec, vmem, vmem, any_spec],
-        out_specs=(any_spec, any_spec, gw_spec, vmem),
-        scratch_shapes=[
-            pltpu.VMEM(tokens.shape, BF),
-            pltpu.VMEM(tokens.shape, BF),
-            pltpu.VMEM((rows, depth), BF),
-            pltpu.VMEM((rows, width), BF),
-            pltpu.VMEM(w_shape, BF),
-            pltpu.VMEM((rows, 3 * width), F32),
-            pltpu.VMEM((rows, 2 * LANES), F32),
-            pltpu.VMEM((rows, 3 * width), BF),
-            pltpu.VMEM((rows, LANES), F32),
-            pltpu.VMEM((block, block), BF),
-            pltpu.VMEM((block, block), BF),
-            pltpu.VMEM((block, 2 * LANES), BF),
-            pltpu.VMEM(c_shape, F32),
-            pltpu.VMEM((span, 3 * seqs, width), F32),
-            pltpu.VMEM((4, seqs, width), F32),
-            dma((2,)),
-            dma(w_sems),
-            dma((2,)),
-            dma((n_chunks, span - 1)),
-            dma((n_chunks, span - 1)),
-            dma((2,)),
-            dma((2,)),
-        ]
-        + links,
+        out_specs=(vmem, vmem, gw_spec, vmem),
+        scratch_shapes=list(held.values()),
         compiler_params=pltpu.CompilerParams(
-            collective_id=0, has_side_effects=True, vmem_limit_bytes=62 << 20
+            collective_id=0, has_side_effects=True, vmem_limit_bytes=VMEM_BYTES
         ),
         name="layer",
-    )(tokens, weights, bias.reshape(1, -1), resets, upstream)
+    )(tokens, weights, bias, resets, upstream)
     if not fused:
         gw = lax.psum_scatter(gw, ("seq", "dp"), scatter_dimension=0, tiled=True)
         gb = lax.psum(gb, ("seq", "dp"))
-    return hid, gtok, gw, gb[0]
+    return hid, gtok, gw, gb
 
 
 def solution(mesh):

time: 119 us -> 105 us (0.88)
  Pallas kernels: 110 us -> 99.6 us
  local copies, waits for them, and re-layouts: 7.17 us -> 4.31 us
  other arithmetic: 1.32 us -> 0 us
    pallas_call x1, Pallas kernels: 110 us -> 99.6 us  [per_device(): pl.pallas_call(functools.partial(layer_kernel, span, peers, fused, chunks...]
    unnamed x7 -> x8, local copies, waits for them, and re-layouts: 5.87 us -> 4.31 us
    pallas_call x1 -> x0, other arithmetic: 1.32 us -> none  [per_device(): pl.pallas_call(functools.partial(layer_kernel, span, peers, fused, chunks...]
    reshape x1 -> x0, local copies, waits for them, and re-layouts: 1.3 us -> none  [per_device(): bias.reshape(1, -1)]
where the time goes in v3:
time: 105 us
  Pallas kernels  99.6 us (95%)
  local copies, waits for them, and re-layouts  4.31 us (4%)
    pallas_call x1, Pallas kernels, per_device(): pl.pallas_call(functools.partial(layer_kernel, span, peers, fused, chunks...  99.6 us
    unnamed x8, local copies, waits for them, and re-layouts  4.31 us

profile of v3, /device:TPU:0, one launch (start us, length us, event | category | flops | bytes accessed | tf_op | source)
XLA Modules:
  0.0 104.6 jit_solution(989280628630564031)
XLA Ops:
  0.6 99.6 %layer.1 = (bf16[8,256,640]{2,1,0:T(8,128)(2,1)S(1)}, bf16[8,256,640]{2,1,0:T(8,128)(2,1)S(1)}, f32[40,1920]{1,0:T(8,128)}, f32[1920]{0:T(1024)}) custom-call(bf16[8,256,640]{2,1,0:T(8,128)(2,1)} %tok.1, bf16[40,1920]{1,0:T(8,128)(2,1)} %wts.1, f32[1920]{0:T(1024)} %bias.1, s32[8,256]{1,0:T(8,128)} %resets.1, bf16[8,256,640]{2,1,0:T(8,128)(2,1)} %up.1), custom_call_target="tpu_custom_call" | custom-call | tf_op jit(solution)/shard_map/layer/pallas_call | solution.py:756
  100.2 1.5 %copy.13 = bf16[8,256,640]{2,1,0:T(8,128)(2,1)} copy(bf16[8,256,640]{2,1,0:T(8,128)(2,1)S(1)} %get-tuple-element.4) | data formatting | bytes 5242880
  101.7 0.0 copy-start
  101.7 0.0 copy-start.1
  101.7 1.5 %copy.14 = bf16[8,256,640]{2,1,0:T(8,128)(2,1)} copy(bf16[8,256,640]{2,1,0:T(8,128)(2,1)S(1)} %get-tuple-element.5) | data formatting | bytes 5242880
  103.2 0.0 copy-done
  103.2 0.7 copy.15
  104.0 0.0 copy-done.1
  104.0 0.6 copy.16
Async XLA Ops:
  101.7 1.5 %copy-start = (f32[40,1920]{1,0:T(8,128)S(1)}, f32[40,1920]{1,0:T(8,128)}, u32[]{:S(2)}) copy-start(f32[40,1920]{1,0:T(8,128)} %get-tuple-element.14) | copy-start | bytes 921604
  101.7 2.2 %copy-start.1 = (f32[1920]{0:T(1024)S(1)}, f32[1920]{0:T(1024)}, u32[]{:S(2)}) copy-start(f32[1920]{0:T(1024)} %get-tuple-element.15) | copy-start | bytes 23044

commit v4 on v3

--- a/solution.py
+++ b/solution.py
@@ -16,6 +16,7 @@
 STEPS = 32
 TWO = 16
 VMEM_BYTES = 56 << 20
+EARLY = 16
 
 
 def cut_chunks(width):
@@ -72,10 +73,14 @@
     shard = slab // 2
     over = -(-shard // 16) * 16
     partner = (me, col ^ 1)
+    pieces = [(c, 0, TRIO) for c in range(len(chunks))]
+    if fused:
+        pieces[-1:] = [(len(chunks) - 1, 2 * LANES, LANES), (len(chunks) - 1, 0, 2 * LANES)]
     if fused:
         own16, pair, sb1, rb1, rb2 = held.own16, held.pair, held.sb1, held.rb1, held.rb2
         own2, rb3, fin, fin_rx, gbs = held.own2, held.rb3, held.fin, held.fin_rx, held.gbs
         a0_sem, a3_sem, r4_sem = held.a0_sem, held.a3_sem, held.r4_sem
+        b1_send, b1_recv, b2_send, b2_recv = held.b1_send, held.b1_recv, held.b2_send, held.b2_recv
         a1_send, a1_recv, a2_send, a2_recv = held.a1_send, held.a1_recv, held.a2_send, held.a2_recv
         r1_send, r1_recv, r2_send, r2_recv = held.r1_send, held.r1_recv, held.r2_send, held.r2_recv
         r3_send, r3_recv, gb_send, gb_recv = held.r3_send, held.r3_recv, held.gb_send, held.gb_recv
@@ -115,13 +120,29 @@
         count, r0, c0 = carried(c, who)
         return wv.at[planes, places, pl.ds(r0, count), pl.ds(c0, TRIO)]
 
+    def early(c, places):
+        _, r0, c0 = carried(c, core)
+        return wv.at[me, places, pl.ds(r0, EARLY), pl.ds(c0, TRIO)]
+
+    def rest(c, planes):
+        count, r0, c0 = carried(c, core)
+        return wv.at[planes, place, pl.ds(mult(r0 + EARLY, 16), count - EARLY), pl.ds(c0, TRIO)]
+
     def a1(c, x):
-        here = part(c, core, me, place)
+        here = rest(c, me)
         return remote(here, here, a1_send.at[c, x - 1], a1_recv.at[c, x - 1], (me ^ x, col))
 
     def a2(c, y):
-        here = part(c, core, slice(None), place)
+        here = rest(c, slice(None))
         return remote(here, here, a2_send.at[c, y - 1], a2_recv.at[c, y - 1], (me, col ^ (2 * y)))
+
+    def b1(c, y):
+        here = early(c, place)
+        return remote(here, here, b1_send.at[c, y - 1], b1_recv.at[c, y - 1], (me, col ^ (2 * y)))
+
+    def b2(c, x):
+        here = early(c, slice(None))
+        return remote(here, here, b2_send.at[c, x - 1], b2_recv.at[c, x - 1], (me ^ x, col))
 
     def a3(c):
         if chunks[c][1] == LANES:
@@ -131,6 +152,31 @@
         else:
             here = part(c, core, slice(None), slice(None))
         return remote(here, here, a3_sem.at[c, 0], a3_sem.at[c, 1], partner)
+
+    def early_go(c):
+        for y in range(1, plane):
+            b1(c, y).wait_recv()
+        for x in range(1, span):
+            b2(c, x).start()
+
+    def plane_go(c):
+        for x in range(1, span):
+            a1(c, x).wait_recv()
+        if c < n_chunks - 1:
+            for x in range(1, span):
+                a1(c + 1, x).start()
+        for y in range(1, plane):
+            if c:
+                a2(c - 1, y).wait_send()
+        for y in range(1, plane):
+            a2(c, y).start()
+
+    def cores_go(c):
+        for y in range(1, plane):
+            a2(c, y).wait_recv()
+        for x in range(1, span):
+            b2(c, x).wait_recv()
+        a3(c).start()
 
     def w_copies(c):
         at, cw = chunks[c]
@@ -171,8 +217,11 @@
                     both = jnp.where(core == 0, both[:count], both[slab - count :])
                 to = pl.ds(mult(left + g * LANES, LANES), LANES)
                 wv[me, place, pl.ds(top, count), to] = both.astype(BF)
-            for x in range(1, span):
-                a1(c, x).start()
+            if c == 0:
+                for x in range(1, span):
+                    a1(0, x).start()
+            for y in range(1, plane):
+                b1(c, y).start()
 
     keep = 1.0 - resets[...].astype(F32)
     tiled = jnp.broadcast_to(keep[None], (STEPS, seqs, steps)).reshape(block, steps)
@@ -202,10 +251,9 @@
 
     in_u.wait()
     if fused:
-        for x in range(1, span):
-            a1(0, x).wait_recv()
-        for y in range(1, plane):
-            a2(0, y).start()
+        early_go(0)
+        plane_go(0)
+        early_go(1)
 
     def stage(b, last):
         at = mult(b * block, block)
@@ -296,7 +344,7 @@
             here, here, sum_send.at[c, k - 1], sum_recv.at[c, k - 1], (lax.rem(me + k, span), col)
         )
 
-    def pass_b(c):
+    def pass_b(c, between=()):
         at, cw = chunks[c]
         halves = range(cw // LANES)
         for k in range(1, span):
@@ -353,6 +401,9 @@
         zeros = tuple(zero for _ in halves)
         _, sum_o = lax.fori_loop(0, blocks, forward, (tuple(enter), zeros))
 
+        for step in between:
+            step()
+
         def backward(n, carry):
             heads, sums_z, sums_f = (list(v) for v in carry)
             r0 = mult((blocks - 1 - n) * block, block)
@@ -397,22 +448,27 @@
             for h in range(cw // LANES)
         ]
 
-    def pass_c(c, turn):
+    def pass_c(p, turn):
+        c, lane, lanes = pieces[p]
         at, cw = chunks[c]
         if fused:
             r0 = mult(((me // (span // 2)) ^ 1 ^ turn) * half_rows, LANES)
-            if c:
-                r1_copy(c - 1, turn).wait_send()
-            result = dot_rows(joined[:, pl.ds(r0, half_rows)], gp[c][...])
-            result = result.reshape(-1, slab, 3 * cw)
+            if p and pieces[p - 1][0] != c:
+                r1_copy(p - 1, turn).wait_send()
+            right = [
+                gp[c][:, h * TRIO + lane : h * TRIO + lane + lanes] for h in range(cw // LANES)
+            ]
+            result = dot_rows(joined[:, pl.ds(r0, half_rows)], jnp.concatenate(right, axis=1))
+            result = result.reshape(-1, slab, result.shape[-1])
             count = carried(c, 0)[0]
             if cw == LANES:
                 zero, one = result[:, :count], result[:, slab - count :]
             else:
-                zero, one = result[:, :, :TRIO], result[:, :, TRIO:]
-            cbuf[turn, :, :count] = jnp.where(core == 0, zero, one)
-            sb1[turn, :, :count] = jnp.where(core == 0, one, zero).astype(BF)
-            r1_copy(c, turn).start()
+                zero, one = result[:, :, :lanes], result[:, :, lanes:]
+            cols = slice(lane, lane + lanes)
+            cbuf[turn, :, :count, cols] = jnp.where(core == 0, zero, one)
+            sb1[turn, :, :count, cols] = jnp.where(core == 0, one, zero).astype(BF)
+            r1_copy(p, turn).start()
         else:
             if c:
                 for copy in gw_copies(c - 1, turn):
@@ -423,96 +479,99 @@
             for copy in gw_copies(c, turn):
                 copy.start()
 
-    def part_rows(c):
-        return pl.ds(0, carried(c, 0)[0])
+    def spot(p):
+        c, lane, lanes = pieces[p]
+        return c, pl.ds(0, carried(c, 0)[0]), pl.ds(lane, lanes)
 
     def orders(turn):
         half = span // 2
         return list(range(half, span)) if turn == 0 else list(range(half - 1, -1, -1))
 
-    def r1_copy(c, turn):
-        k = part_rows(c)
+    def r1_copy(p, turn):
+        c, k, l = spot(p)
         return remote(
-            sb1.at[turn, :, k], rb1.at[c, turn, :, k], r1_send.at[c, turn], r1_recv.at[c, turn],
-            partner,
+            sb1.at[turn, :, k, l], rb1.at[c, turn, :, k, l],
+            r1_send.at[p, turn], r1_recv.at[p, turn], partner,
         )
 
-    def r2_copy(c, turn, n, y):
-        k = part_rows(c)
+    def r2_copy(p, turn, n, y):
+        c, k, l = spot(p)
         x = orders(turn)[n]
         index = ((me ^ x) % (span // 2)) * plane + (place ^ y)
         return remote(
-            rb1.at[c, turn, index, k], rb2.at[c, turn, n, y - 1, k],
-            r2_send.at[c, turn, n, y - 1], r2_recv.at[c, turn, n, y - 1], (me, col ^ (2 * y)),
+            rb1.at[c, turn, index, k, l], rb2.at[c, turn, n, y - 1, k, l],
+            r2_send.at[p, turn, n, y - 1], r2_recv.at[p, turn, n, y - 1], (me, col ^ (2 * y)),
         )
 
-    def r2(c, turn):
-        r1_copy(c, turn).wait_recv()
-        k = part_rows(c)
+    def r2(p, turn):
+        r1_copy(p, turn).wait_recv()
+        c, k, l = spot(p)
         for n, x in enumerate(orders(turn)):
             for y in range(plane - 1, -1, -1):
                 index = ((me ^ x) % (span // 2)) * plane + (place ^ y)
-                total = cbuf[turn, index, k] + rb1[c, turn, index, k].astype(F32)
+                total = cbuf[turn, index, k, l] + rb1[c, turn, index, k, l].astype(F32)
                 if y:
-                    rb1[c, turn, index, k] = total.astype(BF)
-                    r2_copy(c, turn, n, y).start()
+                    rb1[c, turn, index, k, l] = total.astype(BF)
+                    r2_copy(p, turn, n, y).start()
                 else:
-                    own2[c, turn, n, k] = total
-
-    def r3_copy(c, turn, n):
-        k = part_rows(c)
+                    own2[c, turn, n, k, l] = total
+
+    def r3_copy(p, turn, n):
+        c, k, l = spot(p)
         x = orders(turn)[n]
         return remote(
-            rb2.at[c, turn, n, 0, k], rb3.at[c, x - 1, k], r3_send.at[c, x - 1],
-            r3_recv.at[c, x - 1], (me ^ x, col),
+            rb2.at[c, turn, n, 0, k, l], rb3.at[c, x - 1, k, l], r3_send.at[p, x - 1],
+            r3_recv.at[p, x - 1], (me ^ x, col),
         )
 
-    def r3(c, turn):
-        k = part_rows(c)
+    def r3(p, turn):
+        c, k, l = spot(p)
         for n, x in enumerate(orders(turn)):
-            total = own2[c, turn, n, k]
+            total = own2[c, turn, n, k, l]
             for y in range(1, plane):
-                r2_copy(c, turn, n, y).wait_recv()
-                total = total + rb2[c, turn, n, y - 1, k].astype(F32)
+                r2_copy(p, turn, n, y).wait_recv()
+                total = total + rb2[c, turn, n, y - 1, k, l].astype(F32)
             if x:
-                rb2[c, turn, n, 0, k] = total.astype(BF)
-                r3_copy(c, turn, n).start()
+                rb2[c, turn, n, 0, k, l] = total.astype(BF)
+                r3_copy(p, turn, n).start()
             else:
-                own2[c, turn, n, k] = total
-
-    def r4_copy(c):
+                own2[c, turn, n, k, l] = total
+
+    def r4_copy(p):
+        c, _, l = spot(p)
         return remote(
-            fin.at[c, pl.ds(mult(shard * (1 - core), 8), shard)], fin_rx.at[c],
-            r4_sem.at[c, 0], r4_sem.at[c, 1], partner,
+            fin.at[c, pl.ds(mult(shard * (1 - core), 8), shard), l], fin_rx.at[c, :, l],
+            r4_sem.at[p, 0], r4_sem.at[p, 1], partner,
         )
 
-    def put_gw(c, tile, value):
-        at, cw = chunks[c]
-        for g in range(3):
-            lane = mult(g * width + at + tile * LANES, LANES)
+    def put_gw(p, tile, value):
+        c, first, lanes = pieces[p]
+        for g in range(lanes // LANES):
+            gate = first // LANES + g
+            lane = mult(gate * width + chunks[c][0] + tile * LANES, LANES)
             gw[:, pl.ds(lane, LANES)] = value[:, g * LANES : (g + 1) * LANES]
 
-    def each_seq_peer(c):
+    def each_seq_peer():
         return [(turn, n, x) for turn in (0, 1) for n, x in enumerate(orders(turn)) if x]
 
-    def r4(c):
-        k = part_rows(c)
-        total = own2[c, 1, span // 2 - 1, k]
-        for turn, n, x in each_seq_peer(c):
-            r3_copy(c, turn, n).wait_recv()
-            total = total + rb3[c, x - 1, k].astype(F32)
-        fin[c, k] = total
+    def r4(p):
+        c, k, l = spot(p)
+        total = own2[c, 1, span // 2 - 1, k, l]
+        for turn, n, x in each_seq_peer():
+            r3_copy(p, turn, n).wait_recv()
+            total = total + rb3[c, x - 1, k, l].astype(F32)
+        fin[c, k, l] = total
         if chunks[c][1] == LANES:
             off = (slab - over) * core
-            put_gw(c, 0, fin[c, pl.ds(mult(shard * core - off, 8), shard)])
+            put_gw(p, 0, fin[c, pl.ds(mult(shard * core - off, 8), shard), l])
         else:
-            r4_copy(c).start()
-            put_gw(c, core, fin[c, pl.ds(mult(shard * core, 8), shard)])
-
-    def r5(c):
-        if chunks[c][1] != LANES:
-            r4_copy(c).wait_recv()
-            put_gw(c, 1 - core, fin_rx[c])
+            r4_copy(p).start()
+            put_gw(p, core, fin[c, pl.ds(mult(shard * core, 8), shard), l])
+
+    def r5(p):
+        c, _, l = spot(p)
+        r4_copy(p).wait_recv()
+        put_gw(p, 1 - core, fin_rx[c, :, l])
 
     def gb_stage(stage):
         if stage == 0:
@@ -535,48 +594,50 @@
             total = total + gbs[4 + k]
         gbs[stage + 1] = total
 
-    def gathered(c):
-        if not fused:
+    last = n_chunks - 1
+    if not fused:
+        for c in range(n_chunks):
             for copy in w_copies(c):
                 copy.wait()
-            return
-        for y in range(1, plane):
-            a2(c, y).wait_recv()
-        a3(c).start()
-        if c + 1 < n_chunks:
-            for x in range(1, span):
-                a1(c + 1, x).wait_recv()
-            for y in range(1, plane):
-                a2(c + 1, y).start()
-        a3(c).wait_recv()
-
-    def gates_of(c):
-        gathered(c)
-        pass_a(c)
-
-    last = n_chunks - 1
-    if fused:
+            pass_a(c)
+        for c in range(n_chunks):
+            pass_b(c)
+            pass_c(c, 0)
+            pass_c(c, 1)
+    else:
         gbs[0] = jnp.zeros(gbs.shape[1:], F32)
-    gates_of(0)
-    gates_of(1)
-    for c in range(n_chunks):
-        pass_b(c)
-        if fused and c:
-            r2(c - 1, 1)
-        if fused and c == last:
-            gb_go(0)
-        pass_c(c, 0)
-        if fused and c:
-            r3(c - 1, 0)
-        pass_c(c, 1)
-        if fused:
-            if c:
-                r3(c - 1, 1)
-            r2(c, 0)
-            if c > 1:
-                r4(c - 2)
-        if c + 2 < n_chunks:
-            gates_of(c + 2)
+        plane_go(1)
+        cores_go(0)
+        a3(0).wait_recv()
+        pass_a(0)
+        early_go(2)
+        cores_go(1)
+        plane_go(2)
+        pass_b(0)
+        a3(1).wait_recv()
+        pass_a(1)
+        pass_c(0, 0)
+        cores_go(2)
+        pass_c(0, 1)
+        r2(0, 0)
+        a3(2).wait_recv()
+        pass_a(2)
+        r2(0, 1)
+        pass_b(1, [lambda: r3(0, 0)])
+        pass_c(1, 0)
+        r3(0, 1)
+        pass_c(1, 1)
+        r2(1, 0)
+        pass_b(
+            2, [lambda: r2(1, 1), lambda: pass_c(2, 0), lambda: r4(0), lambda: pass_c(2, 1), lambda: r2(2, 0)]
+        )
+        gb_go(0)
+        r3(1, 0)
+        r2(2, 1)
+        pass_c(3, 0)
+        r3(1, 1)
+        pass_c(3, 1)
+        r2(3, 0)
 
     to_left = remote(edge.at[2], edge.at[3], edge_send.at[1], edge_recv.at[1], (me - 1, col))
 
@@ -598,9 +659,13 @@
 
     def late_links(i):
         plan = {
-            1: [lambda: r2(last, 1), lambda: r5(max(0, last - 2)), lambda: gb_sum(0), lambda: gb_go(1)],
-            3: [lambda: r3(last, 0), lambda: r4(last - 1), lambda: gb_sum(1), lambda: gb_go(2)],
-            5: [lambda: r3(last, 1), lambda: r5(last - 1), lambda: gb_sum(2)],
+            0: [lambda: r2(3, 1), lambda: gb_sum(0), lambda: gb_go(1)],
+            1: [lambda: r3(2, 0)],
+            2: [lambda: r4(1), lambda: r3(2, 1), lambda: gb_sum(1), lambda: gb_go(2)],
+            4: [lambda: r3(3, 0), lambda: r5(1), lambda: gb_sum(2)],
+            5: [lambda: r4(2)],
+            6: [lambda: r3(3, 1)],
+            7: [lambda: r5(2)],
         }
         for when, todo in plan.items():
 
@@ -651,30 +716,34 @@
             for copy in gw_copies(n_chunks - 1, turn):
                 copy.wait()
     else:
-        r4(last)
         for g in range(3 * width // LANES):
             gb[g * LANES : (g + 1) * LANES] = gbs[3, g : g + 1, :].reshape(LANES)
-        r5(last)
+        r4(3)
         a0.wait_send()
         for c in range(n_chunks):
             a3(c).wait_send()
             for x in range(1, span):
                 a1(c, x).wait_send()
+                b2(c, x).wait_send()
             for y in range(1, plane):
-                a2(c, y).wait_send()
+                b1(c, y).wait_send()
+        for y in range(1, plane):
+            a2(last, y).wait_send()
+        for p in range(len(pieces)):
             for turn in (0, 1):
+                if pieces[p][0] == last:
+                    r1_copy(p, turn).wait_send()
                 for n, x in enumerate(orders(turn)):
                     for y in range(1, plane):
-                        r2_copy(c, turn, n, y).wait_send()
+                        r2_copy(p, turn, n, y).wait_send()
                     if x:
-                        r3_copy(c, turn, n).wait_send()
-            if chunks[c][1] != LANES:
-                r4_copy(c).wait_send()
-        for turn in (0, 1):
-            r1_copy(last, turn).wait_send()
+                        r3_copy(p, turn, n).wait_send()
+            if chunks[pieces[p][0]][1] != LANES:
+                r4_copy(p).wait_send()
         for stage_index in range(3):
             for copy, _ in gb_stage(stage_index):
                 copy.wait_send()
+        r5(3)
 
 
 def per_device(tokens, weights, bias, resets, upstream):
@@ -689,7 +758,7 @@
     slab = 2 * shard
     plane = peers // 2
     half = span // 2
-    fused = shard % 8 == 0 and slab % 16 == 0 and n_chunks >= 3 and steps // STEPS >= 6
+    fused = shard % 8 == 0 and slab % 16 == 0 and n_chunks == 3 and steps // STEPS >= 8
     any_spec = pl.BlockSpec(memory_space=pl.ANY)
     vmem = pl.BlockSpec(memory_space=pltpu.VMEM)
     dma = pltpu.SemaphoreType.DMA
@@ -734,14 +803,18 @@
             "a1_recv": dma((n_chunks, span - 1)),
             "a2_send": dma((n_chunks, plane - 1)),
             "a2_recv": dma((n_chunks, plane - 1)),
+            "b1_send": dma((n_chunks, plane - 1)),
+            "b1_recv": dma((n_chunks, plane - 1)),
+            "b2_send": dma((n_chunks, span - 1)),
+            "b2_recv": dma((n_chunks, span - 1)),
             "a3_sem": dma((n_chunks, 2)),
-            "r1_send": dma((n_chunks, 2)),
-            "r1_recv": dma((n_chunks, 2)),
-            "r2_send": dma((n_chunks, 2, half, plane - 1)),
-            "r2_recv": dma((n_chunks, 2, half, plane - 1)),
-            "r3_send": dma((n_chunks, span - 1)),
-            "r3_recv": dma((n_chunks, span - 1)),
-            "r4_sem": dma((n_chunks, 2)),
+            "r1_send": dma((n_chunks + 1, 2)),
+            "r1_recv": dma((n_chunks + 1, 2)),
+            "r2_send": dma((n_chunks + 1, 2, half, plane - 1)),
+            "r2_recv": dma((n_chunks + 1, 2, half, plane - 1)),
+            "r3_send": dma((n_chunks + 1, span - 1)),
+            "r3_recv": dma((n_chunks + 1, span - 1)),
+            "r4_sem": dma((n_chunks + 1, 2)),
             "gb_send": dma((span + plane - 1,)),
             "gb_recv": dma((span + plane - 1,)),
         }

time: 105 us -> 101 us (0.962)
  Pallas kernels: 99.6 us -> 95.8 us
    pallas_call x1, Pallas kernels: 99.6 us -> 95.8 us  [per_device(): pl.pallas_call(functools.partial(layer_kernel, span, peers, fused, chunks...]
where the time goes in v4:
time: 101 us
  Pallas kernels  95.8 us (95%)
  local copies, waits for them, and re-layouts  4.31 us (4%)
    pallas_call x1, Pallas kernels, per_device(): pl.pallas_call(functools.partial(layer_kernel, span, peers, fused, chunks...  95.8 us
    unnamed x8, local copies, waits for them, and re-layouts  4.31 us

profile of v4, /device:TPU:0, one launch (start us, length us, event | category | flops | bytes accessed | tf_op | source)
XLA Modules:
  0.0 100.7 jit_solution(3548511092353769695)
XLA Ops:
  0.6 95.8 %layer.1 = (bf16[8,256,640]{2,1,0:T(8,128)(2,1)S(1)}, bf16[8,256,640]{2,1,0:T(8,128)(2,1)S(1)}, f32[40,1920]{1,0:T(8,128)}, f32[1920]{0:T(1024)}) custom-call(bf16[8,256,640]{2,1,0:T(8,128)(2,1)} %tok.1, bf16[40,1920]{1,0:T(8,128)(2,1)} %wts.1, f32[1920]{0:T(1024)} %bias.1, s32[8,256]{1,0:T(8,128)} %resets.1, bf16[8,256,640]{2,1,0:T(8,128)(2,1)} %up.1), custom_call_target="tpu_custom_call" | custom-call | tf_op jit(solution)/shard_map/layer/pallas_call | solution.py:829
  96.4 1.5 %copy.13 = bf16[8,256,640]{2,1,0:T(8,128)(2,1)} copy(bf16[8,256,640]{2,1,0:T(8,128)(2,1)S(1)} %get-tuple-element.4) | data formatting | bytes 5242880
  97.9 0.0 copy-start
  97.9 0.0 copy-start.1
  97.9 1.5 %copy.14 = bf16[8,256,640]{2,1,0:T(8,128)(2,1)} copy(bf16[8,256,640]{2,1,0:T(8,128)(2,1)S(1)} %get-tuple-element.5) | data formatting | bytes 5242880
  99.4 0.0 copy-done
  99.4 0.7 copy.15
  100.1 0.0 copy-done.1
  100.1 0.6 copy.16
Async XLA Ops:
  97.9 1.5 %copy-start = (f32[40,1920]{1,0:T(8,128)S(1)}, f32[40,1920]{1,0:T(8,128)}, u32[]{:S(2)}) copy-start(f32[40,1920]{1,0:T(8,128)} %get-tuple-element.14) | copy-start | bytes 921604
  97.9 2.2 %copy-start.1 = (f32[1920]{0:T(1024)S(1)}, f32[1920]{0:T(1024)}, u32[]{:S(2)}) copy-start(f32[1920]{0:T(1024)} %get-tuple-element.15) | copy-start | bytes 23044

commit v5 on v4

--- a/solution.py
+++ b/solution.py
@@ -610,10 +610,10 @@
         cores_go(0)
         a3(0).wait_recv()
         pass_a(0)
-        early_go(2)
         cores_go(1)
         plane_go(2)
         pass_b(0)
+        early_go(2)
         a3(1).wait_recv()
         pass_a(1)
         pass_c(0, 0)
@@ -661,10 +661,11 @@
         plan = {
             0: [lambda: r2(3, 1), lambda: gb_sum(0), lambda: gb_go(1)],
             1: [lambda: r3(2, 0)],
-            2: [lambda: r4(1), lambda: r3(2, 1), lambda: gb_sum(1), lambda: gb_go(2)],
-            4: [lambda: r3(3, 0), lambda: r5(1), lambda: gb_sum(2)],
-            5: [lambda: r4(2)],
-            6: [lambda: r3(3, 1)],
+            2: [lambda: r3(2, 1), lambda: gb_sum(1), lambda: gb_go(2)],
+            3: [lambda: r4(1)],
+            4: [lambda: r3(3, 0), lambda: gb_sum(2)],
+            5: [lambda: r3(3, 1), lambda: r5(1)],
+            6: [lambda: r4(2)],
             7: [lambda: r5(2)],
         }
         for when, todo in plan.items():
@@ -831,8 +832,8 @@
         out_shape=(
             vm(tokens.shape, BF),
             vm(tokens.shape, BF),
-            jax.ShapeDtypeStruct(gw_shape, F32),
-            jax.ShapeDtypeStruct((3 * width,), F32),
+            vm(gw_shape, F32) if fused else jax.ShapeDtypeStruct(gw_shape, F32),
+            vm((3 * width,), F32) if fused else jax.ShapeDtypeStruct((3 * width,), F32),
         ),
         in_specs=[any_spec, any_spec, vmem, vmem, any_spec],
         out_specs=(vmem, vmem, gw_spec, vmem),

time: 101 us -> 99.8 us (0.988)
  Pallas kernels: 95.8 us -> 94.3 us
    pallas_call x1, Pallas kernels: 95.8 us -> 94.3 us  [per_device(): pl.pallas_call(functools.partial(layer_kernel, span, peers, fused, chunks...]
    unnamed x8 -> x4, local copies, waits for them, and re-layouts: 4.31 us -> 4.3 us
where the time goes in v5:
time: 99.8 us; the launch traced here: 99.3 us
  Pallas kernels  94.3 us (94%)
  local copies, waits for them, and re-layouts  4.3 us (4%)
    pallas_call x1, Pallas kernels, per_device(): pl.pallas_call(functools.partial(layer_kernel, span, peers, fused, chunks...  94.3 us
    unnamed x4, local copies, waits for them, and re-layouts  4.3 us

profile of v5, /device:TPU:0, one launch (start us, length us, event | category | flops | bytes accessed | tf_op | source)
XLA Modules:
  0.0 99.3 jit_solution(10311285407800859019)
XLA Ops:
  0.6 94.3 %layer.1 = (bf16[8,256,640]{2,1,0:T(8,128)(2,1)S(1)}, bf16[8,256,640]{2,1,0:T(8,128)(2,1)S(1)}, f32[40,1920]{1,0:T(8,128)S(1)}, f32[1920]{0:T(1024)S(1)}) custom-call(bf16[8,256,640]{2,1,0:T(8,128)(2,1)} %tok.1, bf16[40,1920]{1,0:T(8,128)(2,1)} %wts.1, f32[1920]{0:T(1024)} %bias.1, s32[8,256]{1,0:T(8,128)} %resets.1, bf16[8,256,640]{2,1,0:T(8,128)(2,1)} %up.1), custom_call_target="tpu_custom_call" | custom-call | tf_op jit(solution)/shard_map/layer/pallas_call | solution.py:830
  95.0 1.5 %copy.13 = bf16[8,256,640]{2,1,0:T(8,128)(2,1)} copy(bf16[8,256,640]{2,1,0:T(8,128)(2,1)S(1)} %get-tuple-element.4) | data formatting | bytes 5242880
  96.5 0.6 copy.16
  97.1 0.7 copy.15
  97.8 1.5 %copy.14 = bf16[8,256,640]{2,1,0:T(8,128)(2,1)} copy(bf16[8,256,640]{2,1,0:T(8,128)(2,1)S(1)} %get-tuple-element.5) | data formatting | bytes 5242880

commit v6 on v5

--- a/solution.py
+++ b/solution.py
@@ -16,7 +16,7 @@
 STEPS = 32
 TWO = 16
 VMEM_BYTES = 56 << 20
-EARLY = 16
+EARLY = (0, 16, 16)
 
 
 def cut_chunks(width):
@@ -122,11 +122,11 @@
 
     def early(c, places):
         _, r0, c0 = carried(c, core)
-        return wv.at[me, places, pl.ds(r0, EARLY), pl.ds(c0, TRIO)]
+        return wv.at[me, places, pl.ds(r0, EARLY[c]), pl.ds(c0, TRIO)]
 
     def rest(c, planes):
         count, r0, c0 = carried(c, core)
-        return wv.at[planes, place, pl.ds(mult(r0 + EARLY, 16), count - EARLY), pl.ds(c0, TRIO)]
+        return wv.at[planes, place, pl.ds(mult(r0 + EARLY[c], 16), count - EARLY[c]), pl.ds(c0, TRIO)]
 
     def a1(c, x):
         here = rest(c, me)
@@ -154,6 +154,8 @@
         return remote(here, here, a3_sem.at[c, 0], a3_sem.at[c, 1], partner)
 
     def early_go(c):
+        if not EARLY[c]:
+            return
         for y in range(1, plane):
             b1(c, y).wait_recv()
         for x in range(1, span):
@@ -175,7 +177,8 @@
         for y in range(1, plane):
             a2(c, y).wait_recv()
         for x in range(1, span):
-            b2(c, x).wait_recv()
+            if EARLY[c]:
+                b2(c, x).wait_recv()
         a3(c).start()
 
     def w_copies(c):
@@ -220,8 +223,9 @@
             if c == 0:
                 for x in range(1, span):
                     a1(0, x).start()
-            for y in range(1, plane):
-                b1(c, y).start()
+            if EARLY[c]:
+                for y in range(1, plane):
+                    b1(c, y).start()
 
     keep = 1.0 - resets[...].astype(F32)
     tiled = jnp.broadcast_to(keep[None], (STEPS, seqs, steps)).reshape(block, steps)
@@ -725,9 +729,11 @@
             a3(c).wait_send()
             for x in range(1, span):
                 a1(c, x).wait_send()
-                b2(c, x).wait_send()
+                if EARLY[c]:
+                    b2(c, x).wait_send()
             for y in range(1, plane):
-                b1(c, y).wait_send()
+                if EARLY[c]:
+                    b1(c, y).wait_send()
         for y in range(1, plane):
             a2(last, y).wait_send()
         for p in range(len(pieces)):

time: 99.8 us -> 98.4 us (0.986)
  Pallas kernels: 94.3 us -> 93.2 us
    pallas_call x1, Pallas kernels: 94.3 us -> 93.2 us  [per_device(): pl.pallas_call(functools.partial(layer_kernel, span, peers, fused, chunks...]
where the time goes in v6:
time: 98.4 us; the launch traced here: 98.1 us
  Pallas kernels  93.2 us (95%)
  local copies, waits for them, and re-layouts  4.3 us (4%)
    pallas_call x1, Pallas kernels, per_device(): pl.pallas_call(functools.partial(layer_kernel, span, peers, fused, chunks...  93.2 us
    unnamed x4, local copies, waits for them, and re-layouts  4.3 us

profile of v6, /device:TPU:0, one launch (start us, length us, event | category | flops | bytes accessed | tf_op | source)
XLA Modules:
  0.0 98.1 jit_solution(4611851631829941626)
XLA Ops:
  0.6 93.2 %layer.1 = (bf16[8,256,640]{2,1,0:T(8,128)(2,1)S(1)}, bf16[8,256,640]{2,1,0:T(8,128)(2,1)S(1)}, f32[40,1920]{1,0:T(8,128)S(1)}, f32[1920]{0:T(1024)S(1)}) custom-call(bf16[8,256,640]{2,1,0:T(8,128)(2,1)} %tok.1, bf16[40,1920]{1,0:T(8,128)(2,1)} %wts.1, f32[1920]{0:T(1024)} %bias.1, s32[8,256]{1,0:T(8,128)} %resets.1, bf16[8,256,640]{2,1,0:T(8,128)(2,1)} %up.1), custom_call_target="tpu_custom_call" | custom-call | tf_op jit(solution)/shard_map/layer/pallas_call | solution.py:836
  93.8 1.5 %copy.13 = bf16[8,256,640]{2,1,0:T(8,128)(2,1)} copy(bf16[8,256,640]{2,1,0:T(8,128)(2,1)S(1)} %get-tuple-element.4) | data formatting | bytes 5242880
  95.3 0.6 copy.16
  95.9 0.7 copy.15
  96.6 1.5 %copy.14 = bf16[8,256,640]{2,1,0:T(8,128)(2,1)} copy(bf16[8,256,640]{2,1,0:T(8,128)(2,1)S(1)} %get-tuple-element.5) | data formatting | bytes 5242880

commit v7 on v6

--- a/solution.py
+++ b/solution.py
@@ -256,8 +256,8 @@
     in_u.wait()
     if fused:
         early_go(0)
+        early_go(1)
         plane_go(0)
-        early_go(1)
 
     def stage(b, last):
         at = mult(b * block, block)

time: 98.4 us -> 100 us (1.016)
  Pallas kernels: 93.2 us -> 94.9 us
    pallas_call x1, Pallas kernels: 93.2 us -> 94.9 us  [per_device(): pl.pallas_call(functools.partial(layer_kernel, span, peers, fused, chunks...]
where the time goes in v7:
time: 100 us; the launch traced here: 99.9 us
  Pallas kernels  94.9 us (95%)
  local copies, waits for them, and re-layouts  4.3 us (4%)
    pallas_call x1, Pallas kernels, per_device(): pl.pallas_call(functools.partial(layer_kernel, span, peers, fused, chunks...  94.9 us
    unnamed x4, local copies, waits for them, and re-layouts  4.3 us

profile of v7, /device:TPU:0, one launch (start us, length us, event | category | flops | bytes accessed | tf_op | source)
XLA Modules:
  0.0 99.9 jit_solution(8237011845766519745)
XLA Ops:
  0.6 94.9 %layer.1 = (bf16[8,256,640]{2,1,0:T(8,128)(2,1)S(1)}, bf16[8,256,640]{2,1,0:T(8,128)(2,1)S(1)}, f32[40,1920]{1,0:T(8,128)S(1)}, f32[1920]{0:T(1024)S(1)}) custom-call(bf16[8,256,640]{2,1,0:T(8,128)(2,1)} %tok.1, bf16[40,1920]{1,0:T(8,128)(2,1)} %wts.1, f32[1920]{0:T(1024)} %bias.1, s32[8,256]{1,0:T(8,128)} %resets.1, bf16[8,256,640]{2,1,0:T(8,128)(2,1)} %up.1), custom_call_target="tpu_custom_call" | custom-call | tf_op jit(solution)/shard_map/layer/pallas_call | solution.py:836
  95.6 1.5 %copy.13 = bf16[8,256,640]{2,1,0:T(8,128)(2,1)} copy(bf16[8,256,640]{2,1,0:T(8,128)(2,1)S(1)} %get-tuple-element.4) | data formatting | bytes 5242880
  97.1 0.6 copy.16
  97.7 0.7 copy.15
  98.4 1.5 %copy.14 = bf16[8,256,640]{2,1,0:T(8,128)(2,1)} copy(bf16[8,256,640]{2,1,0:T(8,128)(2,1)S(1)} %get-tuple-element.5) | data formatting | bytes 5242880
